TPU v7x, 128 devices: a whole 4x4x4 slice. The times are simulated.
128 devices in a mesh: chan: 16 (over y, z_lo, core), ctx: 8 (over x, z_hi).
Axes of the slice: x: 4, y: 4, z: 4 (z_hi: 2, z_lo: 2; z = z_hi * 2 + z_lo), core: 2. Of those that a mesh axis runs over, the one named last changes fastest.
Arguments:
- grad_out: bfloat16 [16384, 4096], P('ctx', 'chan'), may hold values from -6 to 6
- values: bfloat16 [16384, 4096], P('ctx', 'chan'), may hold values from -0.15625 to 0.15625
- gate: bfloat16 [16384, 4096], P('ctx', 'chan'), may hold values from -6 to 6
- pre_gate: bfloat16 [16384, 4096], P('ctx', 'chan'), may hold values from -6 to 6
- filter_spectrum: float32 [2, 32768, 4096], P(None, 'ctx', 'chan'), may hold values from -6 to 6
- skip: float32 [4096], P('chan'), may hold values from 0.5 to 1.5
Outputs:
- input_grad: float32 [16384, 4096], P('ctx', 'chan')
- gate_grad: bfloat16 [16384, 4096], P('ctx', 'chan')
- filter_grad: float32 [16384, 4096], P('ctx', 'chan')
All inputs are finite; a program needn't handle non-finite values.
Results may differ from a plain program's by a relative error of at most 0.0035.
Values may be sent and summed in bfloat16 or wider, within the bound.
A program may use at most 256 MiB of HBM per device.

v0:
```python
import math
import functools
import numpy as np
import jax
import jax.numpy as jnp
import ml_dtypes
from jax import lax
from jax.experimental import pallas as pl
from jax.experimental.pallas import tpu as pltpu

F32 = jnp.float32
BF16 = jnp.bfloat16
N = 32768
LANE_KR = (0, 2, 1, 3)


def split_np(a):
    hi = a.astype(ml_dtypes.bfloat16)
    lo = (a - hi.astype(np.float64)).astype(ml_dtypes.bfloat16)
    return hi, lo


def tables():
    s = np.arange(512)
    ang = 2 * np.pi * ((s[:, None] * s[None, :]) % 512) / 512
    t = np.concatenate([np.cos(ang), np.sin(ang)], 0)
    hi, lo = split_np(t)
    kap = np.arange(9)[:, None] + 16 * np.array(LANE_KR)[None, :]
    prod = (kap[:, None, :] * s[None, :, None]) % N
    ang = 2 * np.pi * prod / N
    tw = np.concatenate([np.repeat(np.cos(ang), 32, 2), np.repeat(np.sin(ang), 32, 2)], 2).astype(np.float32)
    r = np.repeat(np.arange(4), 32)
    ang = 2 * np.pi * np.arange(9)[:, None] * r[None, :] / 64
    lane = np.stack([np.cos(ang), np.sin(ang)], 1).astype(np.float32)
    rev = np.eye(64)[::-1].astype(ml_dtypes.bfloat16)
    return hi, lo, tw, lane, rev


def lane_consts(rows):
    lanes = lax.broadcasted_iota(jnp.int32, (rows, 128), 1)
    block = lanes // 32
    hi = block >= 2
    odd = (block % 2) == 1
    last = block == 3
    return hi, odd, last


def pair64(x, hi):
    return pltpu.roll(x, 64, 1) + jnp.where(hi, -x, x)


def pair32(x, odd):
    return jnp.where(odd, pltpu.roll(x, 32, 1) - x, x + pltpu.roll(x, 96, 1))


def dft4(re, im, masks):
    hi, odd, last = masks
    re, im = pair64(re, hi), pair64(im, hi)
    re, im = jnp.where(last, im, re), jnp.where(last, -re, im)
    return pair32(re, odd), pair32(im, odd)


def idft4(re, im, masks):
    hi, odd, last = masks
    re, im = pair32(re, odd), pair32(im, odd)
    re, im = jnp.where(last, -im, re), jnp.where(last, re, im)
    return pair64(re, hi), pair64(im, hi)


C = [math.cos(2 * math.pi * q / 16) for q in range(16)]
S = [math.sin(2 * math.pi * q / 16) for q in range(16)]


def dft16_half(x):
    y = [None] * 9
    e = [x[i] + x[i + 4] for i in range(4)]
    f = [x[i] - x[i + 4] for i in range(4)]
    a, b = e[0] + e[2], e[1] + e[3]
    y[0] = (a + b, None)
    y[8] = (a - b, None)
    y[4] = (e[0] - e[2], e[3] - e[1])
    g, h = C[2] * (f[1] - f[3]), C[2] * (f[1] + f[3])
    y[2] = (f[0] + g, -(f[2] + h))
    y[6] = (f[0] - g, f[2] - h)
    d = [None] + [x[i] - x[8 - i] for i in (1, 2, 3)]
    s = [None] + [x[i] + x[8 - i] for i in (1, 2, 3)]
    for k in (1, 3):
        p = x[0] + d[2] * C[2 * k % 16]
        q = d[1] * C[k] + d[3] * C[3 * k % 16]
        u = s[1] * S[k] + s[3] * S[3 * k % 16]
        v = s[2] * S[2 * k % 16] + x[4] * S[4 * k % 16]
        y[k] = (p + q, -(u + v))
        y[8 - k] = (p - q, v - u)
    return y


def idft16_half(z):
    a, b = z[0][0] + z[8][0], z[0][0] - z[8][0]
    r4, i4 = z[4]
    e = [a + r4, b - i4, a - r4, b + i4]
    (r2, i2), (r6, i6) = z[2], z[6]
    m, n = r2 - r6, i2 + i6
    f = [r2 + r6, C[2] * (m - n), i6 - i2, -C[2] * (m + n)]
    out = [e[i] + f[i] for i in range(4)] + [e[i] - f[i] for i in range(4)]
    u = [0.0] * 5
    v = [0.0] * 5
    for k in (1, 3):
        rp, rm = z[k][0] + z[8 - k][0], z[k][0] - z[8 - k][0]
        ip, im = z[k][1] + z[8 - k][1], z[k][1] - z[8 - k][1]
        u[0] = u[0] + rp
        v[4] = v[4] + im * S[4 * k % 16]
        for q in (1, 2, 3):
            odd = q % 2 == 1
            u[q] = u[q] + (rm if odd else rp) * C[q * k % 16]
            v[q] = v[q] + (ip if odd else im) * S[q * k % 16]
    out[0] = out[0] + u[0]
    out[4] = out[4] - v[4]
    for q in (1, 2, 3):
        out[q] = out[q] + u[q] - v[q]
        out[8 - q] = out[8 - q] - u[q] - v[q]
    return out


TILE = 16


def fwd_vector(x_ref, u_ref, tw_ref, lane_ref):
    masks = lane_consts(TILE)

    def step(i, _):
        row = pl.multiple_of(i * TILE, TILE)
        rows = pl.ds(row, TILE)
        low = pl.ds(row + 512, TILE)
        y = dft16_half([x_ref[q, rows, :].astype(F32) for q in range(8)])
        for k in range(9):
            re, im = y[k]
            if k:
                lc, ls = lane_ref[k, 0:1, :], lane_ref[k, 1:2, :]
                if im is None:
                    re, im = re * lc, -(re * ls)
                else:
                    re, im = re * lc + im * ls, im * lc - re * ls
            else:
                im = jnp.zeros_like(re)
            re, im = dft4(re, im, masks)
            tc, ts = tw_ref[k, rows, 0:128], tw_ref[k, rows, 128:256]
            re, im = re * tc + im * ts, im * tc - re * ts
            for part, at in ((re, 0), (im, 128)):
                high = part.astype(BF16)
                u_ref[k, rows, at : at + 128] = high
                u_ref[k, low, at : at + 128] = (part - high.astype(F32)).astype(BF16)
        return 0

    lax.fori_loop(0, 512 // TILE, step, 0)


def inv_vector(z_ref, tw_ref, lane_ref, emit, edge, scale):
    masks = lane_consts(TILE)

    def step(i, _):
        row = pl.multiple_of(i * TILE, TILE)
        rows = pl.ds(row, TILE)
        z = []
        for k in range(9):
            re, im = z_ref[k, rows, 0:128], z_ref[k, rows, 128:256]
            tc, ts = tw_ref[k, rows, 0:128], tw_ref[k, rows, 128:256]
            re, im = re * tc - im * ts, im * tc + re * ts
            re, im = idft4(re, im, masks)
            if k:
                lc, ls = lane_ref[k, 0:1, :], lane_ref[k, 1:2, :]
                re, im = re * lc - im * ls, im * lc + re * ls
            if k in (0, 8) and edge != 1.0:
                re = re * edge
            z.append((re, im))
        for q, value in enumerate(idft16_half(z)):
            emit(rows, q, value * scale)
        return 0

    lax.fori_loop(0, 512 // TILE, step, 0)


def matrix_stage(hi_ref, lo_ref, data):
    out = jnp.dot(hi_ref[...], data[...], preferred_element_type=F32)
    out = out + jnp.dot(lo_ref[...], data[0:512, :], preferred_element_type=F32)
    return out


def forward_block(hi_ref, lo_ref, u):
    out = matrix_stage(hi_ref, lo_ref, u)
    c, s = out[0:512], out[512:1024]
    return c[:, 0:128] + s[:, 128:256], c[:, 128:256] - s[:, 0:128]


def inverse_block(hi_ref, lo_ref, g_ref):
    out = matrix_stage(hi_ref, lo_ref, g_ref)
    c, s = out[0:512], out[512:1024]
    return c[:, 0:128] - s[:, 128:256], c[:, 128:256] + s[:, 0:128]


def put_split(ref, re, im):
    for part, at in ((re, 0), (im, 128)):
        high = part.astype(BF16)
        ref[0:512, at : at + 128] = high
        ref[512:1024, at : at + 128] = (part - high.astype(F32)).astype(BF16)


def corr_kernel(dy_ref, v_ref, hi_ref, lo_ref, tw_ref, lane_ref, spec_ref, out_ref, u_ref, z_ref, g_ref):
    fwd_vector(dy_ref, u_ref.at[0], tw_ref, lane_ref)
    fwd_vector(v_ref, u_ref.at[1], tw_ref, lane_ref)

    def block(k, _):
        dr, di = forward_block(hi_ref, lo_ref, u_ref.at[0, k])
        spec_ref[k, :, 0:128] = dr
        spec_ref[k, :, 128:256] = di
        vr, vi = forward_block(hi_ref, lo_ref, u_ref.at[1, k])
        put_split(g_ref, vr * dr + vi * di, vr * di - vi * dr)
        zr, zi = inverse_block(hi_ref, lo_ref, g_ref)
        z_ref[k, :, 0:128] = zr
        z_ref[k, :, 128:256] = zi
        return 0

    lax.fori_loop(0, 9, block, 0)

    def emit(rows, q, value):
        out_ref[q, rows, :] = value.astype(BF16)

    inv_vector(z_ref, tw_ref, lane_ref, emit, 0.5, 2.0 / N)


def conv_kernel(spec_ref, h_ref, hi_ref, lo_ref, tw_ref, lane_ref, out_ref, z_ref, g_ref):
    def block(k, _):
        mirror = jnp.where(k == 0, 0, 16 - k)
        both = jnp.where((k == 0) | (k == 8), 0.0, 1.0)
        for p in range(8):
            rows = pl.ds(64 * p, 64)
            low = pl.ds(512 + 64 * p, 64)
            mr = h_ref[7 - p, 0, mirror].astype(F32) * both
            mi = h_ref[7 - p, 1, mirror].astype(F32) * both
            hr = h_ref[p, 0, k].astype(F32) + mr
            hi = h_ref[p, 1, k].astype(F32) - mi
            dr, di = spec_ref[k, rows, 0:128], spec_ref[k, rows, 128:256]
            for part, at in ((hr * dr + hi * di, 0), (hr * di - hi * dr, 128)):
                high = part.astype(BF16)
                g_ref[rows, at : at + 128] = high
                g_ref[low, at : at + 128] = (part - high.astype(F32)).astype(BF16)
        zr, zi = inverse_block(hi_ref, lo_ref, g_ref)
        z_ref[k, :, 0:128] = zr
        z_ref[k, :, 128:256] = zi
        return 0

    lax.fori_loop(0, 9, block, 0)

    def emit(rows, q, value):
        out_ref[q, rows, :] = value.astype(BF16)

    inv_vector(z_ref, tw_ref, lane_ref, emit, 1.0, 1.0 / N)


def swap_blocks(blocks):
    rows = blocks[0].shape[0]
    hi, odd, _ = lane_consts(rows)
    b = list(blocks)
    for i in (0, 1):
        x, y = b[i], b[i + 2]
        b[i] = jnp.where(hi, pltpu.roll(y, 64, 1), x)
        b[i + 2] = jnp.where(hi, y, pltpu.roll(x, 64, 1))
    for i in (0, 2):
        x, y = b[i], b[i + 1]
        b[i] = jnp.where(odd, pltpu.roll(y, 32, 1), x)
        b[i + 1] = jnp.where(odd, y, pltpu.roll(x, 96, 1))
    return b


def pack_tokens_kernel(grad_ref, gate_ref, val_ref, out_ref):
    def step(i, _):
        row = pl.multiple_of(i * TILE, TILE)
        for half in range(2):
            lanes = slice(128 * half, 128 * half + 128)
            at = [pl.ds(512 * r + row, TILE) for r in range(4)]
            dy = [grad_ref[a, lanes].astype(F32) * gate_ref[a, lanes].astype(F32) for a in at]
            va = [val_ref[a, lanes].astype(F32) for a in at]
            for j, group in enumerate((dy, va)):
                for e, value in enumerate(swap_blocks(group)):
                    out_ref[4 * half + e, j, pl.ds(row, TILE), :] = value.astype(BF16)
        return 0

    lax.fori_loop(0, 512 // TILE, step, 0)


def pack_spectrum_kernel(hbm_ref, rev_ref, out_ref, h_ref, sems):
    copies = [
        pltpu.make_async_copy(hbm_ref.at[ri, :, pl.ds(128 * half, 128)], h_ref.at[ri, half], sems.at[ri, half])
        for ri in range(2)
        for half in range(2)
    ]
    for c in copies:
        c.start()
    for c in copies:
        c.wait()

    def plain(kq, _):
        for ri in range(2):
            for half in range(2):
                blocks = [h_ref[ri, half, pl.ds(kq + 16 * kr, 64, stride=64), :] for kr in LANE_KR]
                for e, value in enumerate(swap_blocks(blocks)):
                    out_ref[4 * half + e, ri, kq] = value.astype(BF16)
        return 0

    def mirrored(kq, _):
        for ri in range(2):
            for half in range(2):
                blocks = [h_ref[ri, half, pl.ds(kq + 16 * kr, 64, stride=64), :] for kr in LANE_KR[::-1]]
                wide = jnp.concatenate([value.astype(BF16) for value in swap_blocks(blocks)], 1)
                wide = jnp.dot(rev_ref[...], wide, preferred_element_type=F32).astype(BF16)
                for e in range(4):
                    out_ref[4 * half + e, ri, kq] = wide[:, 128 * e : 128 * e + 128]
        return 0

    lax.fori_loop(0, 9, plain, 0)
    lax.fori_loop(9, 16, mirrored, 0)


def unpack_kernel(conv_ref, corr_ref, grad_ref, gate_ref, pre_ref, skip_ref, in_ref, gg_ref, fg_ref):
    def step(i, _):
        row = pl.multiple_of(i * TILE, TILE)
        for half in range(2):
            lanes = slice(128 * half, 128 * half + 128)
            at = [pl.ds(512 * r + row, TILE) for r in range(4)]
            conv = swap_blocks([conv_ref[4 * half + e, pl.ds(row, TILE), :].astype(F32) for e in range(4)])
            corr = swap_blocks([corr_ref[4 * half + e, pl.ds(row, TILE), :].astype(F32) for e in range(4)])
            skip = skip_ref[:, lanes]
            for r in range(4):
                g = grad_ref[at[r], lanes].astype(F32)
                in_ref[at[r], lanes] = conv[r] + skip * (g * gate_ref[at[r], lanes].astype(F32))
                gg_ref[at[r], lanes] = (g * pre_ref[at[r], lanes].astype(F32)).astype(BF16)
                fg_ref[at[r], lanes] = corr[r]
        return 0

    lax.fori_loop(0, 512 // TILE, step, 0)


VMEM = pl.BlockSpec(memory_space=pltpu.VMEM)
PARAMS = pltpu.CompilerParams(vmem_limit_bytes=56 << 20)


def call(body, outs, ins, scratch=(), anys=()):
    return pl.pallas_call(
        body,
        out_shape=outs,
        in_specs=[pl.BlockSpec(memory_space=pl.ANY) if i in anys else VMEM for i in range(len(ins))],
        out_specs=jax.tree.map(lambda _: VMEM, outs),
        scratch_shapes=list(scratch),
        compiler_params=PARAMS,
    )(*ins)


def on_device(grad_out, values, gate, pre_gate, filter_spectrum, skip):
    S_ = jax.ShapeDtypeStruct
    hi, lo, tw, lane, rev = tables()
    hi2 = jnp.asarray(np.concatenate([hi, hi], 1))
    lo, tw, lane, rev = (jnp.asarray(a) for a in (lo, tw, lane, rev))
    tokens = call(pack_tokens_kernel, S_((8, 2, 512, 128), BF16), (grad_out, gate, values))
    tokens = lax.all_to_all(tokens, "ctx", 0, 0, tiled=True)
    packed = call(pack_spectrum_kernel, S_((8, 2, 16, 64, 128), BF16), (filter_spectrum, rev),
        (pltpu.VMEM((2, 2, 4096, 128), F32), pltpu.SemaphoreType.DMA((2, 2))), (0,))
    spectrum = lax.all_to_all(packed, "ctx", 0, 0, tiled=True)
    spec, corr = call(
        corr_kernel,
        (S_((9, 512, 256), F32), S_((8, 512, 128), BF16)),
        (tokens[:, 0], tokens[:, 1], hi2, lo, tw, lane),
        (pltpu.VMEM((2, 9, 1024, 256), BF16), pltpu.VMEM((9, 512, 256), F32), pltpu.VMEM((1024, 256), BF16)),
    )
    corr = lax.all_to_all(corr, "ctx", 0, 0, tiled=True)
    conv = call(
        conv_kernel,
        S_((8, 512, 128), BF16),
        (spec, spectrum, hi2, lo, tw, lane),
        (pltpu.VMEM((9, 512, 256), F32), pltpu.VMEM((1024, 256), BF16)),
    )
    conv = lax.all_to_all(conv, "ctx", 0, 0, tiled=True)
    return tuple(
        call(
            unpack_kernel,
            (S_((2048, 256), F32), S_((2048, 256), BF16), S_((2048, 256), F32)),
            (conv, corr, grad_out, gate, pre_gate, skip.reshape(1, 256)),
        )
    )


def solution(mesh):
    from jax.sharding import PartitionSpec as P
    rows = P("ctx", "chan")
    return jax.shard_map(
        on_device,
        mesh=mesh,
        in_specs=(rows, rows, rows, rows, P(None, "ctx", "chan"), P("chan")),
        out_specs=(rows, rows, rows),
        check_vma=False,
    )
```

profile of v0, /device:TPU:22, one launch (start us, length us, event | category | flops | bytes accessed | tf_op | source)
XLA Modules:
  0.0 186.1 jit_solution(18234100654099319554)
XLA Ops:
  0.6 8.6 %shard_map.130 = bf16[8,2,512,128]{3,2,1,0:T(8,128)(2,1)} custom-call(bf16[2048,256]{1,0:T(8,128)(2,1)} %grad_ref.3, bf16[2048,256]{1,0:T(8,128)(2,1)} %gate_ref.3, bf16[2048,256]{1,0:T(8,128)(2,1)} %val_ref.1), custom_call_target="tpu_custom_call" | custom-call | tf_op jit(solution)/shard_map/pallas_call | solution.py:347
  9.3 8.1 %all-to-all-start = ((bf16[8,2,512,128]{3,2,1,0:T(8,128)(2,1)}), bf16[8,2,512,128]{3,2,1,0:T(8,128)(2,1)S(1)}, u32[]{:S(2)}, u32[]{:S(2)}) async-start(bf16[8,2,512,128]{3,2,1,0:T(8,128)(2,1)} %shard_map.130), calls=%async_computation | async-start | bytes 4194304 | tf_op jit(solution)/shard_map/all_to_all | solution.py:363
  17.4 15.9 %shard_map.132 = bf16[8,2,16,64,128]{4,3,2,1,0:T(8,128)(2,1)} custom-call(f32[2,4096,256]{2,1,0:T(8,128)} %hbm_ref.1, bf16[64,64]{1,0:T(8,128)(2,1)} %constant.14.clone.rev_ref), custom_call_target="tpu_custom_call" | custom-call | tf_op jit(solution)/shard_map/pallas_call | solution.py:347
  33.2 11.9 %all-to-all-done = bf16[8,2,512,128]{3,2,1,0:T(8,128)(2,1)S(1)} async-done(((bf16[8,2,512,128]{3,2,1,0:T(8,128)(2,1)}), bf16[8,2,512,128]{3,2,1,0:T(8,128)(2,1)S(1)}, u32[]{:S(2)}, u32[]{:S(2)}) %all-to-all-start) | async-done | bytes 2097184 | tf_op jit(solution)/shard_map/all_to_all | solution.py:363
  45.2 7.8 %all-to-all-start.1 = ((bf16[8,2,16,64,128]{4,3,2,1,0:T(8,128)(2,1)}), bf16[8,2,16,64,128]{4,3,2,1,0:T(8,128)(2,1)}, u32[]{:S(2)}, u32[]{:S(2)}) async-start(bf16[8,2,16,64,128]{4,3,2,1,0:T(8,128)(2,1)} %shard_map.132), calls=%async_computation.1 | async-start | bytes 8388608 | tf_op jit(solution)/shard_map/all_to_all | solution.py:366
  53.0 1.5 slice_bitcast_fusion
  54.4 68.9 %shard_map.131 = (f32[9,512,256]{2,1,0:T(8,128)}, bf16[8,512,128]{2,1,0:T(8,128)(2,1)}) custom-call(bf16[8,512,128]{2,1,0:T(8,128)(2,1)} %get-tuple-element.8.dy_ref, bf16[8,512,128]{2,1,0:T(8,128)(2,1)} %get-tuple-element.7.v_ref, bf16[1024,1024]{1,0:T(8,128)(2,1)} %constant.10.clone.hi_ref, bf16[1024,512]{1,0:T(8,128)(2,1)} %constant.11.clone.lo_ref, ...), custom_call_target="tpu_custom_call" | custom-call | tf_op jit(solution)/shard_map/pallas_call | solution.py:347
  123.3 0.0 all-to-all-done.1.h_ref
  123.3 7.2 %all-to-all-start.3 = ((bf16[8,512,128]{2,1,0:T(8,128)(2,1)}), bf16[8,512,128]{2,1,0:T(8,128)(2,1)S(1)}, u32[]{:S(2)}, u32[]{:S(2)}) async-start(bf16[8,512,128]{2,1,0:T(8,128)(2,1)} %get-tuple-element.6), calls=%async_computation.3 | async-start | bytes 2097152 | tf_op jit(solution)/shard_map/all_to_all | solution.py:373
  130.5 25.5 %shard_map.133 = bf16[8,512,128]{2,1,0:T(8,128)(2,1)} custom-call(f32[9,512,256]{2,1,0:T(8,128)} %get-tuple-element.5.spec_ref, bf16[8,2,16,64,128]{4,3,2,1,0:T(8,128)(2,1)} %all-to-all-done.1.h_ref, bf16[1024,1024]{1,0:T(8,128)(2,1)} %constant.10.clone.hi_ref, bf16[1024,512]{1,0:T(8,128)(2,1)} %constant.11.clone.lo_ref, ...), custom_call_target="tpu_custom_call" | custom-call | tf_op jit(solution)/shard_map/pallas_call | solution.py:347
  156.0 0.0 all-to-all-done.3.corr_ref
  156.0 0.0 copy-start
  156.0 20.2 %all_to_all.20.conv_ref = bf16[8,512,128]{2,1,0:T(8,128)(2,1)} all-to-all(bf16[8,512,128]{2,1,0:T(8,128)(2,1)} %shard_map.133), channel_id=1, replica_groups=mesh['chan'=16,'ctx'=8] {'ctx'}, dimensions={0} | all-to-all | bytes 2097152 | tf_op jit(solution)/shard_map/all_to_all | solution.py:380
  176.2 0.0 copy-done
  176.2 9.9 %shard_map.134 = (f32[2048,256]{1,0:T(8,128)}, bf16[2048,256]{1,0:T(8,128)(2,1)}, f32[2048,256]{1,0:T(8,128)}) custom-call(bf16[8,512,128]{2,1,0:T(8,128)(2,1)} %all_to_all.20.conv_ref, bf16[8,512,128]{2,1,0:T(8,128)(2,1)} %copy-done, bf16[2048,256]{1,0:T(8,128)(2,1)} %grad_ref.3, bf16[2048,256]{1,0:T(8,128)(2,1)} %gate_ref.3, bf16[2048,256]{1,0:T(8,128)(2,1)} %pre_ref.1, ...), custom_call_target="tpu_custom_call" | custom-call | tf_op jit(solution)/shard_map/pallas_call | solution.py:347
Async XLA Ops:
  9.3 35.9 %all-to-all-start = ((bf16[8,2,512,128]{3,2,1,0:T(8,128)(2,1)}), bf16[8,2,512,128]{3,2,1,0:T(8,128)(2,1)S(1)}, u32[]{:S(2)}, u32[]{:S(2)}) async-start(bf16[8,2,512,128]{3,2,1,0:T(8,128)(2,1)} %shard_map.130), calls=%async_computation | async-start | bytes 4194304 | tf_op jit(solution)/shard_map/all_to_all | solution.py:363
  45.2 78.1 %all-to-all-start.1 = ((bf16[8,2,16,64,128]{4,3,2,1,0:T(8,128)(2,1)}), bf16[8,2,16,64,128]{4,3,2,1,0:T(8,128)(2,1)}, u32[]{:S(2)}, u32[]{:S(2)}) async-start(bf16[8,2,16,64,128]{4,3,2,1,0:T(8,128)(2,1)} %shard_map.132), calls=%async_computation.1 | async-start | bytes 8388608 | tf_op jit(solution)/shard_map/all_to_all | solution.py:366
  123.3 32.7 %all-to-all-start.3 = ((bf16[8,512,128]{2,1,0:T(8,128)(2,1)}), bf16[8,512,128]{2,1,0:T(8,128)(2,1)S(1)}, u32[]{:S(2)}, u32[]{:S(2)}) async-start(bf16[8,512,128]{2,1,0:T(8,128)(2,1)} %get-tuple-element.6), calls=%async_computation.3 | async-start | bytes 2097152 | tf_op jit(solution)/shard_map/all_to_all | solution.py:373
  156.0 20.2 %copy-start = (bf16[8,512,128]{2,1,0:T(8,128)(2,1)}, bf16[8,512,128]{2,1,0:T(8,128)(2,1)S(1)}, u32[]{:S(2)}) copy-start(bf16[8,512,128]{2,1,0:T(8,128)(2,1)S(1)} %all-to-all-done.3.corr_ref) | copy-start | bytes 3145732
where the time goes:
time: 188 us; the launch traced here: 186 us
  Pallas kernels  129 us (69%)
  starting transfers between devices  23.1 us (12%)
  blocking collectives  20.2 us (11%)
  waiting for transfers between devices  11.9 us (6%)
    pallas_call x5, Pallas kernels, call(): pl.pallas_call(body, out_shape=outs, in_specs=[pl.BlockSpec(memory_space=...  129 us
    all_to_all x1, blocking collectives, on_device(): conv = lax.all_to_all(conv, 'ctx', 0, 0, tiled=True)  20.2 us
    all_to_all x1, waiting for transfers between devices, on_device(): tokens = lax.all_to_all(tokens, 'ctx', 0, 0, tiled=True)  11.9 us
    all_to_all x1, starting transfers between devices, on_device(): tokens = lax.all_to_all(tokens, 'ctx', 0, 0, tiled=True)  8.09 us
    all_to_all x1, starting transfers between devices, on_device(): spectrum = lax.all_to_all(packed, 'ctx', 0, 0, tiled=True)  7.82 us
    all_to_all x1, starting transfers between devices, on_device(): corr = lax.all_to_all(corr, 'ctx', 0, 0, tiled=True)  7.2 us
  transfers between devices with their start and end apart: 3, of which 1 were waited for; matrix products, arithmetic and copies ran while one was open for 1% of the time, Pallas kernels for 59%

commit v1 on v0

--- a/solution.py
+++ b/solution.py
@@ -5,6 +5,7 @@
 import jax.numpy as jnp
 import ml_dtypes
 from jax import lax
+from jax.sharding import PartitionSpec as P
 from jax.experimental import pallas as pl
 from jax.experimental.pallas import tpu as pltpu
 
@@ -162,7 +163,8 @@
         rows = pl.ds(row, TILE)
         z = []
         for k in range(9):
-            re, im = z_ref[k, rows, 0:128], z_ref[k, rows, 128:256]
+            re = z_ref[pl.ds(1024 * k + row, TILE), :]
+            im = z_ref[pl.ds(1024 * k + 512 + row, TILE), :]
             tc, ts = tw_ref[k, rows, 0:128], tw_ref[k, rows, 128:256]
             re, im = re * tc - im * ts, im * tc + re * ts
             re, im = idft4(re, im, masks)
@@ -202,58 +204,6 @@
         high = part.astype(BF16)
         ref[0:512, at : at + 128] = high
         ref[512:1024, at : at + 128] = (part - high.astype(F32)).astype(BF16)
-
-
-def corr_kernel(dy_ref, v_ref, hi_ref, lo_ref, tw_ref, lane_ref, spec_ref, out_ref, u_ref, z_ref, g_ref):
-    fwd_vector(dy_ref, u_ref.at[0], tw_ref, lane_ref)
-    fwd_vector(v_ref, u_ref.at[1], tw_ref, lane_ref)
-
-    def block(k, _):
-        dr, di = forward_block(hi_ref, lo_ref, u_ref.at[0, k])
-        spec_ref[k, :, 0:128] = dr
-        spec_ref[k, :, 128:256] = di
-        vr, vi = forward_block(hi_ref, lo_ref, u_ref.at[1, k])
-        put_split(g_ref, vr * dr + vi * di, vr * di - vi * dr)
-        zr, zi = inverse_block(hi_ref, lo_ref, g_ref)
-        z_ref[k, :, 0:128] = zr
-        z_ref[k, :, 128:256] = zi
-        return 0
-
-    lax.fori_loop(0, 9, block, 0)
-
-    def emit(rows, q, value):
-        out_ref[q, rows, :] = value.astype(BF16)
-
-    inv_vector(z_ref, tw_ref, lane_ref, emit, 0.5, 2.0 / N)
-
-
-def conv_kernel(spec_ref, h_ref, hi_ref, lo_ref, tw_ref, lane_ref, out_ref, z_ref, g_ref):
-    def block(k, _):
-        mirror = jnp.where(k == 0, 0, 16 - k)
-        both = jnp.where((k == 0) | (k == 8), 0.0, 1.0)
-        for p in range(8):
-            rows = pl.ds(64 * p, 64)
-            low = pl.ds(512 + 64 * p, 64)
-            mr = h_ref[7 - p, 0, mirror].astype(F32) * both
-            mi = h_ref[7 - p, 1, mirror].astype(F32) * both
-            hr = h_ref[p, 0, k].astype(F32) + mr
-            hi = h_ref[p, 1, k].astype(F32) - mi
-            dr, di = spec_ref[k, rows, 0:128], spec_ref[k, rows, 128:256]
-            for part, at in ((hr * dr + hi * di, 0), (hr * di - hi * dr, 128)):
-                high = part.astype(BF16)
-                g_ref[rows, at : at + 128] = high
-                g_ref[low, at : at + 128] = (part - high.astype(F32)).astype(BF16)
-        zr, zi = inverse_block(hi_ref, lo_ref, g_ref)
-        z_ref[k, :, 0:128] = zr
-        z_ref[k, :, 128:256] = zi
-        return 0
-
-    lax.fori_loop(0, 9, block, 0)
-
-    def emit(rows, q, value):
-        out_ref[q, rows, :] = value.astype(BF16)
-
-    inv_vector(z_ref, tw_ref, lane_ref, emit, 1.0, 1.0 / N)
 
 
 def swap_blocks(blocks):
@@ -269,55 +219,6 @@
         b[i] = jnp.where(odd, pltpu.roll(y, 32, 1), x)
         b[i + 1] = jnp.where(odd, y, pltpu.roll(x, 96, 1))
     return b
-
-
-def pack_tokens_kernel(grad_ref, gate_ref, val_ref, out_ref):
-    def step(i, _):
-        row = pl.multiple_of(i * TILE, TILE)
-        for half in range(2):
-            lanes = slice(128 * half, 128 * half + 128)
-            at = [pl.ds(512 * r + row, TILE) for r in range(4)]
-            dy = [grad_ref[a, lanes].astype(F32) * gate_ref[a, lanes].astype(F32) for a in at]
-            va = [val_ref[a, lanes].astype(F32) for a in at]
-            for j, group in enumerate((dy, va)):
-                for e, value in enumerate(swap_blocks(group)):
-                    out_ref[4 * half + e, j, pl.ds(row, TILE), :] = value.astype(BF16)
-        return 0
-
-    lax.fori_loop(0, 512 // TILE, step, 0)
-
-
-def pack_spectrum_kernel(hbm_ref, rev_ref, out_ref, h_ref, sems):
-    copies = [
-        pltpu.make_async_copy(hbm_ref.at[ri, :, pl.ds(128 * half, 128)], h_ref.at[ri, half], sems.at[ri, half])
-        for ri in range(2)
-        for half in range(2)
-    ]
-    for c in copies:
-        c.start()
-    for c in copies:
-        c.wait()
-
-    def plain(kq, _):
-        for ri in range(2):
-            for half in range(2):
-                blocks = [h_ref[ri, half, pl.ds(kq + 16 * kr, 64, stride=64), :] for kr in LANE_KR]
-                for e, value in enumerate(swap_blocks(blocks)):
-                    out_ref[4 * half + e, ri, kq] = value.astype(BF16)
-        return 0
-
-    def mirrored(kq, _):
-        for ri in range(2):
-            for half in range(2):
-                blocks = [h_ref[ri, half, pl.ds(kq + 16 * kr, 64, stride=64), :] for kr in LANE_KR[::-1]]
-                wide = jnp.concatenate([value.astype(BF16) for value in swap_blocks(blocks)], 1)
-                wide = jnp.dot(rev_ref[...], wide, preferred_element_type=F32).astype(BF16)
-                for e in range(4):
-                    out_ref[4 * half + e, ri, kq] = wide[:, 128 * e : 128 * e + 128]
-        return 0
-
-    lax.fori_loop(0, 9, plain, 0)
-    lax.fori_loop(9, 16, mirrored, 0)
 
 
 def unpack_kernel(conv_ref, corr_ref, grad_ref, gate_ref, pre_ref, skip_ref, in_ref, gg_ref, fg_ref):
@@ -354,30 +255,238 @@
     )(*ins)
 
 
+MESH = pl.DeviceIdType.MESH
+OFFSETS = ((2, 1), (2, 0), (1, 1), (3, 1), (1, 0), (3, 0), (0, 1))
+SLOT = {}
+for _i, _k in enumerate((0, 8, 1, 15, 2, 14, 3, 13, 4, 12, 5, 11, 6, 10, 7, 9)):
+    SLOT[_k] = _i
+SPEC = 9 * 1024
+
+
+def pack_dy(grad_ref, gate_ref, out_ref):
+    def step(i, _):
+        row = pl.multiple_of(i * TILE, TILE)
+        for half in range(2):
+            lanes = slice(128 * half, 128 * half + 128)
+            at = [pl.ds(512 * r + row, TILE) for r in range(4)]
+            dy = [grad_ref[a, lanes].astype(F32) * gate_ref[a, lanes].astype(F32) for a in at]
+            for e, value in enumerate(swap_blocks(dy)):
+                out_ref[4 * half + e, pl.ds(row, TILE), :] = value.astype(BF16)
+        return 0
+
+    lax.fori_loop(0, 512 // TILE, step, 0)
+
+
+def pack_values(val_ref, out_ref):
+    def step(i, _):
+        row = pl.multiple_of(i * TILE, TILE)
+        for half in range(2):
+            lanes = slice(128 * half, 128 * half + 128)
+            va = [val_ref[pl.ds(512 * r + row, TILE), lanes].astype(F32) for r in range(4)]
+            for e, value in enumerate(swap_blocks(va)):
+                out_ref[4 * half + e, pl.ds(row, TILE), :] = value.astype(BF16)
+        return 0
+
+    lax.fori_loop(0, 512 // TILE, step, 0)
+
+
+def pack_plain(h_ref, out_ref, kq, slot):
+    for ri in range(2):
+        for half in range(2):
+            base = (2 * ri + half) * 4096 + kq
+            blocks = [h_ref[pl.ds(base + 16 * kr, 64, stride=64), :] for kr in LANE_KR]
+            for e, value in enumerate(swap_blocks(blocks)):
+                out_ref[4 * half + e, slot, ri] = value.astype(BF16)
+
+
+def pack_mirrored(h_ref, rev_ref, out_ref, kq, slot):
+    for ri in range(2):
+        for half in range(2):
+            base = (2 * ri + half) * 4096 + kq
+            blocks = [h_ref[pl.ds(base + 16 * kr, 64, stride=64), :] for kr in LANE_KR[::-1]]
+            wide = jnp.concatenate([value.astype(BF16) for value in swap_blocks(blocks)], 1)
+            wide = jnp.dot(rev_ref[...], wide, preferred_element_type=F32).astype(BF16)
+            for e in range(4):
+                out_ref[4 * half + e, slot, ri] = wide[:, 128 * e : 128 * e + 128]
+
+
+def pack_spectrum(h_ref, rev_ref, out_ref, chunk):
+    if chunk == 0:
+        pack_plain(h_ref, out_ref, 0, 0)
+        pack_plain(h_ref, out_ref, 8, 1)
+        pack_plain(h_ref, out_ref, 1, 2)
+        pack_mirrored(h_ref, rev_ref, out_ref, 15, 3)
+        return
+
+    def step(i, _):
+        k = 2 * chunk + i
+        pack_plain(h_ref, out_ref, k, 4 * chunk + 2 * i)
+        pack_mirrored(h_ref, rev_ref, out_ref, 16 - k, 4 * chunk + 2 * i + 1)
+        return 0
+
+    lax.fori_loop(0, 2, step, 0)
+
+
+def conv_block(big_ref, h_ref, hi_ref, lo_ref, g_ref, k, slot, mirror):
+    for p in range(8):
+        rows = pl.ds(64 * p, 64)
+        low = pl.ds(512 + 64 * p, 64)
+        hr = h_ref[p, slot, 0].astype(F32)
+        hi = h_ref[p, slot, 1].astype(F32)
+        if mirror is not None:
+            hr = hr + h_ref[7 - p, mirror, 0].astype(F32)
+            hi = hi - h_ref[7 - p, mirror, 1].astype(F32)
+        dr = big_ref[pl.ds(SPEC + 1024 * k + 64 * p, 64), :]
+        di = big_ref[pl.ds(SPEC + 1024 * k + 512 + 64 * p, 64), :]
+        for part, at in ((hr * dr + hi * di, 0), (hr * di - hi * dr, 128)):
+            high = part.astype(BF16)
+            g_ref[rows, at : at + 128] = high
+            g_ref[low, at : at + 128] = (part - high.astype(F32)).astype(BF16)
+    zr, zi = inverse_block(hi_ref, lo_ref, g_ref)
+    big_ref[pl.ds(1024 * k, 512), :] = zr
+    big_ref[pl.ds(1024 * k + 512, 512), :] = zi
+
+
+def main_kernel(
+    grad_hbm, gate_hbm, val_hbm, h_hbm, hi_hbm, lo_hbm, tw_hbm, lane_ref, rev_ref,
+    corr_out, conv_out,
+    grad_v, gate_v, val_v, hi_v, lo_v, tw_v, tok_send, tok_recv, h_send, h_recv,
+    big, u_ref, g_ref, res_send, load_sems, own_sems, send_sems, recv_sems,
+):
+    me = lax.axis_index("ctx")
+    x, z = me // 2, me % 2
+    peers = [((x + dx) % 4) * 2 + (z + dz) % 2 for dx, dz in OFFSETS]
+
+    loads = [(grad_hbm, grad_v), (gate_hbm, gate_v), (val_hbm, val_v)]
+    for ri in range(2):
+        for half in range(2):
+            loads.append((h_hbm.at[ri, :, pl.ds(128 * half, 128)], big.at[pl.ds((2 * ri + half) * 4096, 4096), :]))
+    loads += [(tw_hbm, tw_v), (hi_hbm, hi_v), (lo_hbm, lo_v)]
+    loads = [pltpu.make_async_copy(a, b, load_sems.at[i]) for i, (a, b) in enumerate(loads)]
+    for c in loads:
+        c.start()
+    barrier = pltpu.get_barrier_semaphore()
+    for peer in peers:
+        pl.semaphore_signal(barrier, inc=1, device_id={"ctx": peer}, device_id_type=MESH)
+
+    def exchange(group, source, target):
+        copies = []
+        for i, peer in enumerate(peers):
+            c = pltpu.make_async_remote_copy(
+                src_ref=source(peer), dst_ref=target,
+                send_sem=send_sems.at[group, i], recv_sem=recv_sems.at[group, i],
+                device_id={"ctx": peer}, device_id_type=MESH,
+            )
+            c.start()
+            copies.append(c)
+        own = pltpu.make_async_copy(source(me), target, own_sems.at[group])
+        own.start()
+        return copies, own
+
+    def arrived(pair):
+        for c in pair[0]:
+            c.wait_recv()
+        pair[1].wait()
+
+    loads[0].wait()
+    loads[1].wait()
+    pack_dy(grad_v, gate_v, tok_send.at[0])
+    pl.semaphore_wait(barrier, 7)
+    dy_move = exchange(0, lambda d: tok_send.at[0, d], tok_recv.at[0, me])
+    loads[2].wait()
+    pack_values(val_v, tok_send.at[1])
+    val_move = exchange(1, lambda d: tok_send.at[1, d], tok_recv.at[1, me])
+    for c in loads[3:7]:
+        c.wait()
+    h_moves = []
+    for chunk in range(4):
+        pack_spectrum(big, rev_ref, h_send, chunk)
+        part = pl.ds(4 * chunk, 4)
+        h_moves.append(exchange(2 + chunk, lambda d: h_send.at[d, part], h_recv.at[me, part]))
+    for c in loads[7:]:
+        c.wait()
+
+    arrived(dy_move)
+    fwd_vector(tok_recv.at[0], u_ref.at[0], tw_v, lane_ref)
+    arrived(val_move)
+    fwd_vector(tok_recv.at[1], u_ref.at[1], tw_v, lane_ref)
+
+    def block(k, _):
+        dr, di = forward_block(hi_v, lo_v, u_ref.at[0, k])
+        big[pl.ds(SPEC + 1024 * k, 512), :] = dr
+        big[pl.ds(SPEC + 1024 * k + 512, 512), :] = di
+        vr, vi = forward_block(hi_v, lo_v, u_ref.at[1, k])
+        put_split(g_ref, vr * dr + vi * di, vr * di - vi * dr)
+        zr, zi = inverse_block(hi_v, lo_v, g_ref)
+        big[pl.ds(1024 * k, 512), :] = zr
+        big[pl.ds(1024 * k + 512, 512), :] = zi
+        return 0
+
+    lax.fori_loop(0, 9, block, 0)
+
+    def emit_to(n):
+        def emit(rows, q, value):
+            res_send[n, q, rows, :] = value.astype(BF16)
+        return emit
+
+    inv_vector(big, tw_v, lane_ref, emit_to(0), 0.5, 2.0 / N)
+    corr_move = exchange(6, lambda d: res_send.at[0, d], corr_out.at[me])
+
+    for chunk in range(4):
+        arrived(h_moves[chunk])
+        if chunk == 0:
+            conv_block(big, h_recv, hi_v, lo_v, g_ref, 0, 0, None)
+            conv_block(big, h_recv, hi_v, lo_v, g_ref, 8, 1, None)
+            conv_block(big, h_recv, hi_v, lo_v, g_ref, 1, 2, 3)
+        else:
+            def step(i, _, chunk=chunk):
+                slot = 4 * chunk + 2 * i
+                conv_block(big, h_recv, hi_v, lo_v, g_ref, 2 * chunk + i, slot, slot + 1)
+                return 0
+            lax.fori_loop(0, 2, step, 0)
+    inv_vector(big, tw_v, lane_ref, emit_to(1), 1.0, 1.0 / N)
+    conv_move = exchange(7, lambda d: res_send.at[1, d], conv_out.at[me])
+    arrived(corr_move)
+    arrived(conv_move)
+    for pair in (dy_move, val_move, *h_moves, corr_move, conv_move):
+        for c in pair[0]:
+            c.wait_send()
+
+
 def on_device(grad_out, values, gate, pre_gate, filter_spectrum, skip):
     S_ = jax.ShapeDtypeStruct
     hi, lo, tw, lane, rev = tables()
     hi2 = jnp.asarray(np.concatenate([hi, hi], 1))
     lo, tw, lane, rev = (jnp.asarray(a) for a in (lo, tw, lane, rev))
-    tokens = call(pack_tokens_kernel, S_((8, 2, 512, 128), BF16), (grad_out, gate, values))
-    tokens = lax.all_to_all(tokens, "ctx", 0, 0, tiled=True)
-    packed = call(pack_spectrum_kernel, S_((8, 2, 16, 64, 128), BF16), (filter_spectrum, rev),
-        (pltpu.VMEM((2, 2, 4096, 128), F32), pltpu.SemaphoreType.DMA((2, 2))), (0,))
-    spectrum = lax.all_to_all(packed, "ctx", 0, 0, tiled=True)
-    spec, corr = call(
-        corr_kernel,
-        (S_((9, 512, 256), F32), S_((8, 512, 128), BF16)),
-        (tokens[:, 0], tokens[:, 1], hi2, lo, tw, lane),
-        (pltpu.VMEM((2, 9, 1024, 256), BF16), pltpu.VMEM((9, 512, 256), F32), pltpu.VMEM((1024, 256), BF16)),
-    )
-    corr = lax.all_to_all(corr, "ctx", 0, 0, tiled=True)
-    conv = call(
-        conv_kernel,
-        S_((8, 512, 128), BF16),
-        (spec, spectrum, hi2, lo, tw, lane),
-        (pltpu.VMEM((9, 512, 256), F32), pltpu.VMEM((1024, 256), BF16)),
-    )
-    conv = lax.all_to_all(conv, "ctx", 0, 0, tiled=True)
+    anywhere = pl.BlockSpec(memory_space=pl.ANY)
+    result = S_((8, 512, 128), BF16)
+    corr, conv = pl.pallas_call(
+        main_kernel,
+        out_shape=(result, result),
+        in_specs=[anywhere] * 7 + [VMEM] * 2,
+        out_specs=(anywhere, anywhere),
+        scratch_shapes=[
+            pltpu.VMEM((2048, 256), BF16),
+            pltpu.VMEM((2048, 256), BF16),
+            pltpu.VMEM((2048, 256), BF16),
+            pltpu.VMEM((1024, 1024), BF16),
+            pltpu.VMEM((1024, 512), BF16),
+            pltpu.VMEM((9, 512, 256), F32),
+            pltpu.VMEM((2, 8, 512, 128), BF16),
+            pltpu.VMEM((2, 8, 512, 128), BF16),
+            pltpu.VMEM((8, 16, 2, 64, 128), BF16),
+            pltpu.VMEM((8, 16, 2, 64, 128), BF16),
+            pltpu.VMEM((18 * 1024, 128), F32),
+            pltpu.VMEM((2, 9, 1024, 256), BF16),
+            pltpu.VMEM((1024, 256), BF16),
+            pltpu.VMEM((2, 8, 512, 128), BF16),
+            pltpu.SemaphoreType.DMA((10,)),
+            pltpu.SemaphoreType.DMA((8,)),
+            pltpu.SemaphoreType.DMA((8, 7)),
+            pltpu.SemaphoreType.DMA((8, 7)),
+        ],
+        compiler_params=pltpu.CompilerParams(collective_id=0, has_side_effects=True, vmem_limit_bytes=58 << 20),
+    )(grad_out, gate, values, filter_spectrum, hi2, lo, tw, lane, rev)
     return tuple(
         call(
             unpack_kernel,
@@ -388,7 +497,6 @@
 
 
 def solution(mesh):
-    from jax.sharding import PartitionSpec as P
     rows = P("ctx", "chan")
     return jax.shard_map(
         on_device,

time: 188 us -> 138 us (0.73)
  starting transfers between devices: 23.1 us -> 0 us
  blocking collectives: 20.2 us -> 0 us
  waiting for transfers between devices: 11.9 us -> 0 us
  Pallas kernels: 129 us -> 137 us
    pallas_call x0 -> x1, Pallas kernels: none -> 127 us  [on_device(): pl.pallas_call(main_kernel, out_shape=(result, result), in_specs=[anywher...]
    pallas_call x5 -> x1, Pallas kernels: 129 us -> 9.92 us  [call(): pl.pallas_call(body, out_shape=outs, in_specs=[pl.BlockSpec(memory_space=...]
    all_to_all x3 -> x0, starting transfers between devices: 23.1 us -> none  [the longest x1 8.09 us: on_device(): tokens = lax.all_to_all(tokens, 'ctx', 0, 0, tiled=True)]
    all_to_all x1 -> x0, blocking collectives: 20.2 us -> none  [on_device(): conv = lax.all_to_all(conv, 'ctx', 0, 0, tiled=True)]
    all_to_all x3 -> x0, waiting for transfers between devices: 11.9 us -> none  [the longest x1 11.9 us: on_device(): tokens = lax.all_to_all(tokens, 'ctx', 0, 0, tiled=True)]
  transfers between devices with their start and end apart: 3 -> 0, of which waited for: 1 -> 0; matrix products, arithmetic and copies ran while one was open for 1% -> 0% of each run, Pallas kernels for 59% -> 0%
where the time goes in v1:
time: 138 us; the launch traced here: 137 us
  Pallas kernels  137 us (99%)
    pallas_call x1, Pallas kernels, on_device(): pl.pallas_call(main_kernel, out_shape=(result, result), in_specs=[anywher...  127 us
    pallas_call x1, Pallas kernels, call(): pl.pallas_call(body, out_shape=outs, in_specs=[pl.BlockSpec(memory_space=...  9.92 us

profile of v1, /device:TPU:22, one launch (start us, length us, event | category | flops | bytes accessed | tf_op | source)
XLA Modules:
  0.0 137.3 jit_solution(11470712312239132894)
XLA Ops:
  0.6 126.7 %shard_map.130 = (bf16[8,512,128]{2,1,0:T(8,128)(2,1)}, bf16[8,512,128]{2,1,0:T(8,128)(2,1)}) custom-call(bf16[2048,256]{1,0:T(8,128)(2,1)} %grad_ref.1, bf16[2048,256]{1,0:T(8,128)(2,1)} %gate_ref.1, bf16[2048,256]{1,0:T(8,128)(2,1)} %val_hbm.1, f32[2,4096,256]{2,1,0:T(8,128)} %h_hbm.1, bf16[1024,1024]{1,0:T(8,128)(2,1)} %constant.10.clone.hi_hbm, ...), custom_call_target="tpu_custom_call" | custom-call | tf_op jit(solution)/shard_map/pallas_call | solution.py:463
  127.4 9.9 %shard_map.131 = (f32[2048,256]{1,0:T(8,128)}, bf16[2048,256]{1,0:T(8,128)(2,1)}, f32[2048,256]{1,0:T(8,128)}) custom-call(bf16[8,512,128]{2,1,0:T(8,128)(2,1)} %get-tuple-element.5.conv_ref, bf16[8,512,128]{2,1,0:T(8,128)(2,1)} %get-tuple-element.6.corr_ref, bf16[2048,256]{1,0:T(8,128)(2,1)} %grad_ref.1, bf16[2048,256]{1,0:T(8,128)(2,1)} %gate_ref.1, ...), custom_call_target="tpu_custom_call" | custom-call | tf_op jit(solution)/shard_map/pallas_call | solution.py:248

commit v2 on v1

v2 whole, which is shorter than its diff:
```python
import math

import numpy as np
import jax
import jax.numpy as jnp
import ml_dtypes
from jax import lax
from jax.experimental import pallas as pl
from jax.experimental.pallas import tpu as pltpu
from jax.sharding import PartitionSpec as P

F32 = jnp.float32
BF16 = jnp.bfloat16
N = 32768


def split_np(a):
    hi = a.astype(ml_dtypes.bfloat16)
    lo = (a - hi.astype(np.float64)).astype(ml_dtypes.bfloat16)
    return hi, lo


def tables():
    s = np.arange(256)
    ang = 2 * np.pi * ((s[:, None] * s[None, :]) % 256) / 256
    hi, lo = split_np(np.concatenate([np.cos(ang), np.sin(ang)], 0))
    kap = np.arange(9)[:, None] + 16 * np.arange(4)[None, :]
    both = np.stack([kap, kap + 64], 1)
    ang = 2 * np.pi * ((both[:, :, None, :] * s[None, None, :, None]) % N) / N
    ang = np.repeat(ang.reshape(9, 512, 4), 32, 2)
    twiddle = np.concatenate([np.cos(ang), np.sin(ang)], 2).astype(np.float32)
    r = np.repeat(np.arange(4), 32)
    ang = 2 * np.pi * np.arange(9)[:, None] * r[None, :] / 64
    half = 2 * np.pi * np.repeat(kap, 32, 1) / 128
    lane = np.stack([np.cos(ang), np.sin(ang), np.cos(half), np.sin(half)], 1)
    lane = np.concatenate([lane, lane], 1).astype(np.float32)
    rr = np.arange(4)
    c = np.kron(np.round(np.cos(np.pi * rr[:, None] * rr[None, :] / 2)), np.eye(32))
    n = np.kron(np.round(np.sin(np.pi * rr[:, None] * rr[None, :] / 2)), np.eye(32))
    fwd = np.block([[c, -n], [n, c]])
    inv = np.block([[c, n], [-n, c]])
    cross = np.stack([np.concatenate([fwd, fwd], 0), np.concatenate([inv, inv], 0)], 0)
    swap = np.eye(512).reshape(4, 4, 32, 512).transpose(1, 0, 2, 3).reshape(512, 512)
    rev = np.eye(64)[::-1]
    cross, swap, rev = (a.astype(ml_dtypes.bfloat16) for a in (cross, swap, rev))
    return np.concatenate([hi, hi], 1), lo, twiddle, lane, cross, swap, rev


C = [math.cos(2 * math.pi * q / 16) for q in range(16)]
S = [math.sin(2 * math.pi * q / 16) for q in range(16)]


def dft16_half(x):
    y = [None] * 9
    e = [x[i] + x[i + 4] for i in range(4)]
    f = [x[i] - x[i + 4] for i in range(4)]
    a, b = e[0] + e[2], e[1] + e[3]
    y[0] = (a + b, None)
    y[8] = (a - b, None)
    y[4] = (e[0] - e[2], e[3] - e[1])
    g, h = C[2] * (f[1] - f[3]), C[2] * (f[1] + f[3])
    y[2] = (f[0] + g, -(f[2] + h))
    y[6] = (f[0] - g, f[2] - h)
    d = [None] + [x[i] - x[8 - i] for i in (1, 2, 3)]
    s = [None] + [x[i] + x[8 - i] for i in (1, 2, 3)]
    for k in (1, 3):
        p = x[0] + d[2] * C[2 * k % 16]
        q = d[1] * C[k] + d[3] * C[3 * k % 16]
        u = s[1] * S[k] + s[3] * S[3 * k % 16]
        v = s[2] * S[2 * k % 16] + x[4] * S[4 * k % 16]
        y[k] = (p + q, -(u + v))
        y[8 - k] = (p - q, v - u)
    return y


def idft16_half(z):
    a, b = z[0][0] + z[8][0], z[0][0] - z[8][0]
    r4, i4 = z[4]
    e = [a + r4, b - i4, a - r4, b + i4]
    (r2, i2), (r6, i6) = z[2], z[6]
    m, n = r2 - r6, i2 + i6
    f = [r2 + r6, C[2] * (m - n), i6 - i2, -C[2] * (m + n)]
    out = [e[i] + f[i] for i in range(4)] + [e[i] - f[i] for i in range(4)]
    u = [0.0] * 5
    v = [0.0] * 5
    for k in (1, 3):
        rp, rm = z[k][0] + z[8 - k][0], z[k][0] - z[8 - k][0]
        ip, im = z[k][1] + z[8 - k][1], z[k][1] - z[8 - k][1]
        u[0] = u[0] + rp
        v[4] = v[4] + im * S[4 * k % 16]
        for q in (1, 2, 3):
            odd = q % 2 == 1
            u[q] = u[q] + (rm if odd else rp) * C[q * k % 16]
            v[q] = v[q] + (ip if odd else im) * S[q * k % 16]
    out[0] = out[0] + u[0]
    out[4] = out[4] - v[4]
    for q in (1, 2, 3):
        out[q] = out[q] + u[q] - v[q]
        out[8 - q] = out[8 - q] - u[q] - v[q]
    return out


TILE = 16


def split(value):
    high = value.astype(BF16)
    return high, (value - high.astype(F32)).astype(BF16)


def forward_q(x_ref, a_ref, lane_ref):
    def step(i, _):
        rows = pl.ds(pl.multiple_of(i * TILE, TILE), TILE)
        y = dft16_half([x_ref[q, rows, :].astype(F32) for q in range(8)])
        for k in range(9):
            re, im = y[k]
            lc, ls = lane_ref[k, 0:1, :], lane_ref[k, 1:2, :]
            if k == 0:
                im = jnp.zeros_like(re)
            elif im is None:
                re, im = re * lc, -(re * ls)
            else:
                re, im = re * lc + im * ls, im * lc - re * ls
            for part, at in ((re, 0), (im, 128)):
                high, low = split(part)
                a_ref[k, rows, at : at + 128] = high
                a_ref[k, rows, at + 256 : at + 384] = low
        return 0

    lax.fori_loop(0, 512 // TILE, step, 0)


def inverse_q(z_ref, emit, edge, scale):
    def step(i, _):
        row = pl.multiple_of(i * TILE, TILE)
        z = []
        for k in range(9):
            re = z_ref[pl.ds(1024 * k + row, TILE), :]
            im = z_ref[pl.ds(1024 * k + 512 + row, TILE), :]
            if k in (0, 8) and edge != 1.0:
                re = re * edge
            z.append((re, im))
        for q, value in enumerate(idft16_half(z)):
            emit(pl.ds(row, TILE), q, value * scale)
        return 0

    lax.fori_loop(0, 512 // TILE, step, 0)


def long_dot(hi_ref, lo_ref, g_ref):
    out = jnp.dot(hi_ref[...], g_ref[...], preferred_element_type=F32)
    out = out + jnp.dot(lo_ref[...], g_ref[0:256, :], preferred_element_type=F32)
    return out[0:256], out[256:512]


def forward_k(a_ref, k, tabs, g_ref):
    hi_ref, lo_ref, tw_ref, lane_ref, cross_ref = tabs
    d = jnp.dot(a_ref[k], cross_ref[0], preferred_element_type=F32)
    r0, i0 = d[0:256, 0:128], d[0:256, 128:256]
    r1, i1 = d[256:512, 0:128], d[256:512, 128:256]
    c, s = lane_ref[k, 2:3, :], lane_ref[k, 3:4, :]
    r1, i1 = r1 * c + i1 * s, i1 * c - r1 * s
    out = []
    for kh, (re, im) in enumerate(((r0 + r1, i0 + i1), (r0 - r1, i0 - i1))):
        c, s = tw_ref[k, 256 * kh : 256 * kh + 256, 0:128], tw_ref[k, 256 * kh : 256 * kh + 256, 128:256]
        re, im = re * c + im * s, im * c - re * s
        put(g_ref.at[kh], slice(0, 256), slice(256, 512), re, im)
        c, s = long_dot(hi_ref, lo_ref, g_ref.at[kh])
        out.append((c[:, 0:128] + s[:, 128:256], c[:, 128:256] - s[:, 0:128]))
    return out


def put(ref, rows, low_rows, re, im):
    for part, at in ((re, 0), (im, 128)):
        high, low = split(part)
        ref[rows, at : at + 128] = high
        ref[low_rows, at : at + 128] = low


def inverse_k(g_ref, k, tabs, a_ref, z_ref):
    hi_ref, lo_ref, tw_ref, lane_ref, cross_ref = tabs
    b = []
    for kh in range(2):
        c, s = long_dot(hi_ref, lo_ref, g_ref.at[kh])
        re, im = c[:, 0:128] - s[:, 128:256], c[:, 128:256] + s[:, 0:128]
        c, s = tw_ref[k, 256 * kh : 256 * kh + 256, 0:128], tw_ref[k, 256 * kh : 256 * kh + 256, 128:256]
        b.append((re * c - im * s, im * c + re * s))
    (r0, i0), (r1, i1) = b
    c, s = lane_ref[k, 2:3, :], lane_ref[k, 3:4, :]
    r1, i1, r0, i0 = r0 - r1, i0 - i1, r0 + r1, i0 + i1
    r1, i1 = r1 * c - i1 * s, i1 * c + r1 * s
    for at, (re, im) in ((0, (r0, i0)), (256, (r1, i1))):
        for part, lanes in ((re, 0), (im, 128)):
            high, low = split(part)
            a_ref[at : at + 256, lanes : lanes + 128] = high
            a_ref[at : at + 256, lanes + 256 : lanes + 384] = low
    d = jnp.dot(a_ref[...], cross_ref[1], preferred_element_type=F32)
    re, im = d[:, 0:128], d[:, 128:256]
    c, s = lane_ref[k, 0:1, :], lane_ref[k, 1:2, :]
    z_ref[pl.ds(1024 * k, 512), :] = re * c - im * s
    z_ref[pl.ds(1024 * k + 512, 512), :] = im * c + re * s


def exchange_groups(blocks, swap_ref):
    return jnp.dot(jnp.concatenate(blocks, 1), swap_ref[...], preferred_element_type=F32)


def unpack_kernel(conv_ref, corr_ref, grad_ref, gate_ref, pre_ref, skip_ref, swap_ref, in_ref, gg_ref, fg_ref):
    for half in range(2):
        lanes = slice(128 * half, 128 * half + 128)
        conv = exchange_groups([conv_ref[4 * half + e] for e in range(4)], swap_ref)
        corr = exchange_groups([corr_ref[4 * half + e] for e in range(4)], swap_ref)
        skip = skip_ref[:, lanes]
        for r in range(4):
            g = grad_ref[r, :, lanes].astype(F32)
            in_ref[r, :, lanes] = conv[:, 128 * r : 128 * r + 128] + skip * (g * gate_ref[r, :, lanes].astype(F32))
            gg_ref[r, :, lanes] = (g * pre_ref[r, :, lanes].astype(F32)).astype(BF16)
            fg_ref[r, :, lanes] = corr[:, 128 * r : 128 * r + 128]


MESH = pl.DeviceIdType.MESH
OFFSETS = ((2, 1), (2, 0), (1, 1), (3, 1), (1, 0), (3, 0), (0, 1))
SPEC = 9 * 1024
PACK = 256


def pack_dy(grad_ref, gate_ref, swap_ref, out_ref):
    def step(i, _):
        row = pl.multiple_of(i * PACK, PACK)
        for half in range(2):
            lanes = slice(128 * half, 128 * half + 128)
            at = [pl.ds(512 * r + row, PACK) for r in range(4)]
            dy = [(grad_ref[a, lanes].astype(F32) * gate_ref[a, lanes].astype(F32)).astype(BF16) for a in at]
            dy = exchange_groups(dy, swap_ref).astype(BF16)
            for e in range(4):
                out_ref[4 * half + e, pl.ds(row, PACK), :] = dy[:, 128 * e : 128 * e + 128]
        return 0

    lax.fori_loop(0, 512 // PACK, step, 0)


def pack_values(val_ref, swap_ref, out_ref):
    def step(i, _):
        row = pl.multiple_of(i * PACK, PACK)
        for half in range(2):
            lanes = slice(128 * half, 128 * half + 128)
            va = exchange_groups([val_ref[pl.ds(512 * r + row, PACK), lanes] for r in range(4)], swap_ref).astype(BF16)
            for e in range(4):
                out_ref[4 * half + e, pl.ds(row, PACK), :] = va[:, 128 * e : 128 * e + 128]
        return 0

    lax.fori_loop(0, 512 // PACK, step, 0)


def pack_rows(h_ref, swap_ref, rev_ref, out_ref, kq, slot, mirrored):
    parts = []
    for ri in range(2):
        for half in range(2):
            base = (2 * ri + half) * 4096 + kq
            blocks = []
            for kr in (3, 2, 1, 0) if mirrored else range(4):
                rows = [h_ref[pl.ds(base + 16 * kr + 64 * kh, 32, stride=128), :] for kh in range(2)]
                blocks.append(jnp.concatenate(rows, 0).astype(BF16))
            parts.append(jnp.concatenate(blocks, 1))
    wide = jnp.dot(jnp.concatenate(parts, 0), swap_ref[...], preferred_element_type=F32).astype(BF16)
    for n in range(4):
        rows = wide[64 * n : 64 * n + 64]
        if mirrored:
            rows = jnp.dot(rev_ref[...], rows, preferred_element_type=F32).astype(BF16)
        for e in range(4):
            out_ref[4 * (n % 2) + e, slot, n // 2] = rows[:, 128 * e : 128 * e + 128]


def pack_spectrum(h_ref, swap_ref, rev_ref, out_ref, chunk):
    if chunk == 0:
        pack_rows(h_ref, swap_ref, rev_ref, out_ref, 0, 0, False)
        pack_rows(h_ref, swap_ref, rev_ref, out_ref, 8, 1, False)
        pack_rows(h_ref, swap_ref, rev_ref, out_ref, 1, 2, False)
        pack_rows(h_ref, swap_ref, rev_ref, out_ref, 15, 3, True)
        return

    def step(i, _):
        k = 2 * chunk + i
        pack_rows(h_ref, swap_ref, rev_ref, out_ref, k, 4 * chunk + 2 * i, False)
        pack_rows(h_ref, swap_ref, rev_ref, out_ref, 16 - k, 4 * chunk + 2 * i + 1, True)
        return 0

    lax.fori_loop(0, 2, step, 0)


def conv_block(big_ref, h_ref, tabs, g_ref, a_ref, k, slot, mirror):
    for kh in range(2):
        for p in range(8):
            at = slice(32 * kh, 32 * kh + 32)
            hr = h_ref[p, slot, 0, at, :].astype(F32)
            hi = h_ref[p, slot, 1, at, :].astype(F32)
            if mirror is not None:
                hr = hr + h_ref[7 - p, mirror, 0, at, :].astype(F32)
                hi = hi - h_ref[7 - p, mirror, 1, at, :].astype(F32)
            first = SPEC + 1024 * k + 256 * kh + 32 * p
            dr, di = big_ref[pl.ds(first, 32), :], big_ref[pl.ds(first + 512, 32), :]
            rows, low = slice(32 * p, 32 * p + 32), slice(256 + 32 * p, 288 + 32 * p)
            put(g_ref.at[kh], rows, low, hr * dr + hi * di, hr * di - hi * dr)
    inverse_k(g_ref, k, tabs, a_ref, big_ref)


def main_kernel(
    grad_hbm, gate_hbm, val_hbm, h_hbm, hi_hbm, lo_hbm, tw_hbm, cross_hbm, swap_hbm, lane_ref, rev_ref,
    corr_out, conv_out,
    grad_v, gate_v, val_v, hi_v, lo_v, tw_v, cross_v, swap_v, tok_send, tok_recv, h_send, h_recv,
    big, dy_a, val_a, inv_a, dy_g, val_g, inv_g, res_send, load_sems, own_sems, send_sems, recv_sems,
):
    me = lax.axis_index("ctx")
    x, z = me // 2, me % 2
    peers = [((x + dx) % 4) * 2 + (z + dz) % 2 for dx, dz in OFFSETS]

    loads = [(grad_hbm, grad_v), (gate_hbm, gate_v), (swap_hbm, swap_v), (val_hbm, val_v)]
    for ri in range(2):
        for half in range(2):
            loads.append((h_hbm.at[ri, :, pl.ds(128 * half, 128)], big.at[pl.ds((2 * ri + half) * 4096, 4096), :]))
    loads += [(tw_hbm, tw_v), (hi_hbm, hi_v), (lo_hbm, lo_v), (cross_hbm, cross_v)]
    loads = [pltpu.make_async_copy(a, b, load_sems.at[i]) for i, (a, b) in enumerate(loads)]
    for c in loads:
        c.start()
    barrier = pltpu.get_barrier_semaphore()
    for peer in peers:
        pl.semaphore_signal(barrier, inc=1, device_id={"ctx": peer}, device_id_type=MESH)

    def exchange(group, source, target):
        copies = []
        for i, peer in enumerate(peers):
            c = pltpu.make_async_remote_copy(
                src_ref=source(peer), dst_ref=target,
                send_sem=send_sems.at[group, i], recv_sem=recv_sems.at[group, i],
                device_id={"ctx": peer}, device_id_type=MESH,
            )
            c.start()
            copies.append(c)
        own = pltpu.make_async_copy(source(me), target, own_sems.at[group])
        own.start()
        return copies, own

    def arrived(pair):
        for c in pair[0]:
            c.wait_recv()
        pair[1].wait()

    loads[0].wait()
    loads[1].wait()
    loads[2].wait()
    pack_dy(grad_v, gate_v, swap_v, tok_send.at[0])
    pl.semaphore_wait(barrier, 7)
    dy_move = exchange(0, lambda d: tok_send.at[0, d], tok_recv.at[0, me])
    loads[3].wait()
    pack_values(val_v, swap_v, tok_send.at[1])
    val_move = exchange(1, lambda d: tok_send.at[1, d], tok_recv.at[1, me])
    for c in loads[4:8]:
        c.wait()
    h_moves = []
    for chunk in range(4):
        pack_spectrum(big, swap_v, rev_ref, h_send, chunk)
        part = pl.ds(4 * chunk, 4)
        h_moves.append(exchange(2 + chunk, lambda d: h_send.at[d, part], h_recv.at[me, part]))
    for c in loads[8:]:
        c.wait()

    tabs = (hi_v, lo_v, tw_v, lane_ref, cross_v)
    arrived(dy_move)
    forward_q(tok_recv.at[0], dy_a, lane_ref)
    arrived(val_move)
    forward_q(tok_recv.at[1], val_a, lane_ref)

    def block(k, _):
        dy_s = forward_k(dy_a, k, tabs, dy_g)
        val_s = forward_k(val_a, k, tabs, val_g)
        for kh in range(2):
            (dr, di), (vr, vi) = dy_s[kh], val_s[kh]
            first = SPEC + 1024 * k + 256 * kh
            big[pl.ds(first, 256), :] = dr
            big[pl.ds(first + 512, 256), :] = di
            put(inv_g.at[kh], slice(0, 256), slice(256, 512), vr * dr + vi * di, vr * di - vi * dr)
        inverse_k(inv_g, k, tabs, inv_a, big)
        return 0

    lax.fori_loop(0, 9, block, 0)

    def emit_to(n):
        def emit(rows, q, value):
            res_send[n, q, rows, :] = value.astype(BF16)
        return emit

    inverse_q(big, emit_to(0), 0.5, 2.0 / N)
    corr_move = exchange(6, lambda d: res_send.at[0, d], corr_out.at[me])

    for chunk in range(4):
        arrived(h_moves[chunk])
        if chunk == 0:
            conv_block(big, h_recv, tabs, inv_g, inv_a, 0, 0, None)
            conv_block(big, h_recv, tabs, inv_g, inv_a, 8, 1, None)
            conv_block(big, h_recv, tabs, inv_g, inv_a, 1, 2, 3)
        else:
            def step(i, _, chunk=chunk):
                slot = 4 * chunk + 2 * i
                conv_block(big, h_recv, tabs, inv_g, inv_a, 2 * chunk + i, slot, slot + 1)
                return 0
            lax.fori_loop(0, 2, step, 0)
    inverse_q(big, emit_to(1), 1.0, 1.0 / N)
    conv_move = exchange(7, lambda d: res_send.at[1, d], conv_out.at[me])
    arrived(corr_move)
    arrived(conv_move)
    for pair in (dy_move, val_move, *h_moves, corr_move, conv_move):
        for c in pair[0]:
            c.wait_send()


def on_device(grad_out, values, gate, pre_gate, filter_spectrum, skip):
    S_ = jax.ShapeDtypeStruct
    hi, lo, tw, lane, cross, swap, rev = (jnp.asarray(a) for a in tables())
    anywhere = pl.BlockSpec(memory_space=pl.ANY)
    vmem = pl.BlockSpec(memory_space=pltpu.VMEM)
    result = S_((8, 512, 128), BF16)
    tokens = pltpu.VMEM((2048, 256), BF16)
    corr, conv = pl.pallas_call(
        main_kernel,
        out_shape=(result, result),
        in_specs=[anywhere] * 9 + [vmem] * 2,
        out_specs=(anywhere, anywhere),
        scratch_shapes=[
            tokens,
            tokens,
            tokens,
            pltpu.VMEM((512, 512), BF16),
            pltpu.VMEM((512, 256), BF16),
            pltpu.VMEM((9, 512, 256), F32),
            pltpu.VMEM((2, 512, 256), BF16),
            pltpu.VMEM((512, 512), BF16),
            pltpu.VMEM((2, 8, 512, 128), BF16),
            pltpu.VMEM((2, 8, 512, 128), BF16),
            pltpu.VMEM((8, 16, 2, 64, 128), BF16),
            pltpu.VMEM((8, 16, 2, 64, 128), BF16),
            pltpu.VMEM((18 * 1024, 128), F32),
            pltpu.VMEM((9, 512, 512), BF16),
            pltpu.VMEM((9, 512, 512), BF16),
            pltpu.VMEM((512, 512), BF16),
            pltpu.VMEM((2, 512, 256), BF16),
            pltpu.VMEM((2, 512, 256), BF16),
            pltpu.VMEM((2, 512, 256), BF16),
            pltpu.VMEM((2, 8, 512, 128), BF16),
            pltpu.SemaphoreType.DMA((12,)),
            pltpu.SemaphoreType.DMA((8,)),
            pltpu.SemaphoreType.DMA((8, 7)),
            pltpu.SemaphoreType.DMA((8, 7)),
        ],
        compiler_params=pltpu.CompilerParams(collective_id=0, has_side_effects=True, vmem_limit_bytes=58 << 20),
    )(grad_out, gate, values, filter_spectrum, hi, lo, tw, cross, swap, lane, rev)

    rows = 128
    packed = pl.BlockSpec((8, rows, 128), lambda i: (0, i, 0))
    plain = pl.BlockSpec((4, rows, 256), lambda i: (0, i, 0))
    whole = lambda shape: pl.BlockSpec(shape, lambda i: (0, 0))
    fold = lambda a: a.reshape(4, 512, 256)
    outs = pl.pallas_call(
        unpack_kernel,
        grid=(512 // rows,),
        out_shape=(S_((4, 512, 256), F32), S_((4, 512, 256), BF16), S_((4, 512, 256), F32)),
        in_specs=[packed, packed, plain, plain, plain, whole((1, 256)), whole((512, 512))],
        out_specs=(plain, plain, plain),
        compiler_params=pltpu.CompilerParams(vmem_limit_bytes=32 << 20),
    )(conv, corr, fold(grad_out), fold(gate), fold(pre_gate), skip.reshape(1, 256), swap)
    return tuple(a.reshape(2048, 256) for a in outs)


def solution(mesh):
    rows = P("ctx", "chan")
    return jax.shard_map(
        on_device,
        mesh=mesh,
        in_specs=(rows, rows, rows, rows, P(None, "ctx", "chan"), P("chan")),
        out_specs=(rows, rows, rows),
        check_vma=False,
    )
```

time: 138 us -> 112 us (0.81)
  Pallas kernels: 137 us -> 107 us
  local copies, waits for them, and re-layouts: 0 us -> 2.47 us
    pallas_call x1, Pallas kernels: 127 us -> 103 us  [on_device(): pl.pallas_call(main_kernel, out_shape=(result, result), in_specs=[anywher...]
    pallas_call x1, Pallas kernels: 9.92 us -> 3.84 us  [on_device(): pl.pallas_call(unpack_kernel, grid=(512 // rows,), out_shape=(S_((4, 512,...]
    unnamed x0 -> x14, local copies, waits for them, and re-layouts: none -> 2.47 us
where the time goes in v2:
time: 112 us; the launch traced here: 110 us
  Pallas kernels  107 us (96%)
  local copies, waits for them, and re-layouts  2.47 us (2%)
    pallas_call x1, Pallas kernels, on_device(): pl.pallas_call(main_kernel, out_shape=(result, result), in_specs=[anywher...  103 us
    pallas_call x1, Pallas kernels, on_device(): pl.pallas_call(unpack_kernel, grid=(512 // rows,), out_shape=(S_((4, 512,...  3.84 us
    unnamed x14, local copies, waits for them, and re-layouts  2.47 us

profile of v2, /device:TPU:22, one launch (start us, length us, event | category | flops | bytes accessed | tf_op | source)
XLA Modules:
  0.0 110.3 jit_solution(12037628985678649682)
XLA Ops:
  0.6 0.0 copy-start
  0.6 0.0 copy-start.1
  0.7 0.0 copy-start.2
  0.7 0.0 copy-start.3
  0.7 0.0 copy-start.6
  0.7 103.3 %shard_map.148 = (bf16[8,512,128]{2,1,0:T(8,128)(2,1)}, bf16[8,512,128]{2,1,0:T(8,128)(2,1)}) custom-call(bf16[2048,256]{1,0:T(8,128)(2,1)} %grad_hbm.1, bf16[2048,256]{1,0:T(8,128)(2,1)} %gate_hbm.1, bf16[2048,256]{1,0:T(8,128)(2,1)} %val_hbm.1, f32[2,4096,256]{2,1,0:T(8,128)} %h_hbm.1, bf16[512,512]{1,0:T(8,128)(2,1)} %constant.14.clone.hi_hbm, ...), custom_call_target="tpu_custom_call" | custom-call | tf_op jit(solution)/shard_map/pallas_call | solution.py:423
  104.0 0.0 copy-done
  104.0 0.0 copy-done.1
  104.0 0.0 copy-done.2
  104.0 0.0 copy-done.3
  104.0 0.0 copy-done.6
  104.0 0.0 copy-start.4
  104.0 1.2 %copy-done.4 = bf16[8,512,128]{2,1,0:T(8,128)(2,1)S(1)} copy-done((bf16[8,512,128]{2,1,0:T(8,128)(2,1)S(1)}, bf16[8,512,128]{2,1,0:T(8,128)(2,1)}, u32[]{:S(2)}) %copy-start.4) | copy-done | bytes 1048600
  105.3 0.0 copy-start.5
  105.3 1.2 %copy-done.5 = bf16[8,512,128]{2,1,0:T(8,128)(2,1)S(1)} copy-done((bf16[8,512,128]{2,1,0:T(8,128)(2,1)S(1)}, bf16[8,512,128]{2,1,0:T(8,128)(2,1)}, u32[]{:S(2)}) %copy-start.5) | copy-done | bytes 1048600
  106.5 3.8 %shard_map.149 = (f32[4,512,256]{2,1,0:T(8,128)}, bf16[4,512,256]{2,1,0:T(8,128)(2,1)}, f32[4,512,256]{2,1,0:T(8,128)}) custom-call(bf16[8,512,128]{2,1,0:T(8,128)(2,1)S(1)} %copy-done.5, bf16[8,512,128]{2,1,0:T(8,128)(2,1)S(1)} %copy-done.4, bf16[4,512,256]{2,1,0:T(8,128)(2,1)S(1)} %bitcast.7, bf16[4,512,256]{2,1,0:T(8,128)(2,1)S(1)} %bitcast.8, ...), custom_call_target="tpu_custom_call" | custom-call | tf_op jit(solution)/shard_map/pallas_call | solution.py:462
Async XLA Ops:
  0.6 103.3 %copy-start = (bf16[2048,256]{1,0:T(8,128)(2,1)S(1)}, bf16[2048,256]{1,0:T(8,128)(2,1)}, u32[]{:S(2)}) copy-start(bf16[2048,256]{1,0:T(8,128)(2,1)} %grad_hbm.1) | copy-start | bytes 3145732
  0.6 103.3 %copy-start.1 = (bf16[2048,256]{1,0:T(8,128)(2,1)S(1)}, bf16[2048,256]{1,0:T(8,128)(2,1)}, u32[]{:S(2)}) copy-start(bf16[2048,256]{1,0:T(8,128)(2,1)} %gate_hbm.1) | copy-start | bytes 3145732
  0.7 103.3 %copy-start.2 = (bf16[512,512]{1,0:T(8,128)(2,1)S(1)}, bf16[512,512]{1,0:T(8,128)(2,1)}, u32[]{:S(2)}) copy-start(bf16[512,512]{1,0:T(8,128)(2,1)} %constant.19.clone.swap_hbm.swap_ref) | copy-start | bytes 1572868
  0.7 103.3 %copy-start.3 = (bf16[2048,256]{1,0:T(8,128)(2,1)S(1)}, bf16[2048,256]{1,0:T(8,128)(2,1)}, u32[]{:S(2)}) copy-start(bf16[2048,256]{1,0:T(8,128)(2,1)} %param.16) | copy-start | bytes 3145732
  0.7 103.3 %copy-start.6 = (f32[256]{0:T(256)S(1)}, f32[256]{0:T(256)}, u32[]{:S(2)}) copy-start(f32[256]{0:T(256)} %param.18) | copy-start | bytes 3076
  104.0 1.2 %copy-start.4 = (bf16[8,512,128]{2,1,0:T(8,128)(2,1)S(1)}, bf16[8,512,128]{2,1,0:T(8,128)(2,1)}, u32[]{:S(2)}) copy-start(bf16[8,512,128]{2,1,0:T(8,128)(2,1)} %get-tuple-element.9.corr_ref) | copy-start | bytes 3145732
  105.3 1.2 %copy-start.5 = (bf16[8,512,128]{2,1,0:T(8,128)(2,1)S(1)}, bf16[8,512,128]{2,1,0:T(8,128)(2,1)}, u32[]{:S(2)}) copy-start(bf16[8,512,128]{2,1,0:T(8,128)(2,1)} %get-tuple-element.8.conv_ref) | copy-start | bytes 3145732

commit v3 on v2

--- a/solution.py
+++ b/solution.py
@@ -108,7 +108,7 @@
     return high, (value - high.astype(F32)).astype(BF16)
 
 
-def forward_q(x_ref, a_ref, lane_ref):
+def forward_q(x_ref, a_ref, lane_ref, part):
     def step(i, _):
         rows = pl.ds(pl.multiple_of(i * TILE, TILE), TILE)
         y = dft16_half([x_ref[q, rows, :].astype(F32) for q in range(8)])
@@ -127,10 +127,10 @@
                 a_ref[k, rows, at + 256 : at + 384] = low
         return 0
 
-    lax.fori_loop(0, 512 // TILE, step, 0)
-
-
-def inverse_q(z_ref, emit, edge, scale):
+    lax.fori_loop(part * (256 // TILE), (part + 1) * (256 // TILE), step, 0)
+
+
+def inverse_q(z_ref, emit, edge, scale, part):
     def step(i, _):
         row = pl.multiple_of(i * TILE, TILE)
         z = []
@@ -144,7 +144,7 @@
             emit(pl.ds(row, TILE), q, value * scale)
         return 0
 
-    lax.fori_loop(0, 512 // TILE, step, 0)
+    lax.fori_loop(part * (256 // TILE), (part + 1) * (256 // TILE), step, 0)
 
 
 def long_dot(hi_ref, lo_ref, g_ref):
@@ -219,37 +219,30 @@
 
 
 MESH = pl.DeviceIdType.MESH
-OFFSETS = ((2, 1), (2, 0), (1, 1), (3, 1), (1, 0), (3, 0), (0, 1))
+OFFSETS = ((2, 0), (0, 1), (2, 1), (1, 1), (3, 0), (3, 1), (1, 0))
+CHUNKS = ((0, 4), (4, 4), (8, 4), (12, 2), (14, 2))
 SPEC = 9 * 1024
 PACK = 256
-
-
-def pack_dy(grad_ref, gate_ref, swap_ref, out_ref):
-    def step(i, _):
-        row = pl.multiple_of(i * PACK, PACK)
-        for half in range(2):
-            lanes = slice(128 * half, 128 * half + 128)
-            at = [pl.ds(512 * r + row, PACK) for r in range(4)]
-            dy = [(grad_ref[a, lanes].astype(F32) * gate_ref[a, lanes].astype(F32)).astype(BF16) for a in at]
-            dy = exchange_groups(dy, swap_ref).astype(BF16)
-            for e in range(4):
-                out_ref[4 * half + e, pl.ds(row, PACK), :] = dy[:, 128 * e : 128 * e + 128]
-        return 0
-
-    lax.fori_loop(0, 512 // PACK, step, 0)
-
-
-def pack_values(val_ref, swap_ref, out_ref):
-    def step(i, _):
-        row = pl.multiple_of(i * PACK, PACK)
-        for half in range(2):
-            lanes = slice(128 * half, 128 * half + 128)
-            va = exchange_groups([val_ref[pl.ds(512 * r + row, PACK), lanes] for r in range(4)], swap_ref).astype(BF16)
-            for e in range(4):
-                out_ref[4 * half + e, pl.ds(row, PACK), :] = va[:, 128 * e : 128 * e + 128]
-        return 0
-
-    lax.fori_loop(0, 512 // PACK, step, 0)
+CORR_AFTER = 3
+
+
+def pack_dy(grad_ref, gate_ref, swap_ref, out_ref, part):
+    for half in range(2):
+        lanes = slice(128 * half, 128 * half + 128)
+        at = [slice(512 * r + PACK * part, 512 * r + PACK * part + PACK) for r in range(4)]
+        dy = [(grad_ref[a, lanes].astype(F32) * gate_ref[a, lanes].astype(F32)).astype(BF16) for a in at]
+        dy = exchange_groups(dy, swap_ref).astype(BF16)
+        for e in range(4):
+            out_ref[4 * half + e, PACK * part : PACK * part + PACK, :] = dy[:, 128 * e : 128 * e + 128]
+
+
+def pack_values(val_ref, swap_ref, out_ref, part):
+    for half in range(2):
+        lanes = slice(128 * half, 128 * half + 128)
+        at = [slice(512 * r + PACK * part, 512 * r + PACK * part + PACK) for r in range(4)]
+        va = exchange_groups([val_ref[a, lanes] for a in at], swap_ref).astype(BF16)
+        for e in range(4):
+            out_ref[4 * half + e, PACK * part : PACK * part + PACK, :] = va[:, 128 * e : 128 * e + 128]
 
 
 def pack_rows(h_ref, swap_ref, rev_ref, out_ref, kq, slot, mirrored):
@@ -272,20 +265,20 @@
 
 
 def pack_spectrum(h_ref, swap_ref, rev_ref, out_ref, chunk):
-    if chunk == 0:
+    first, count = CHUNKS[chunk]
+    if first == 0:
         pack_rows(h_ref, swap_ref, rev_ref, out_ref, 0, 0, False)
         pack_rows(h_ref, swap_ref, rev_ref, out_ref, 8, 1, False)
-        pack_rows(h_ref, swap_ref, rev_ref, out_ref, 1, 2, False)
-        pack_rows(h_ref, swap_ref, rev_ref, out_ref, 15, 3, True)
-        return
+        first, count = 2, count - 2
 
     def step(i, _):
-        k = 2 * chunk + i
-        pack_rows(h_ref, swap_ref, rev_ref, out_ref, k, 4 * chunk + 2 * i, False)
-        pack_rows(h_ref, swap_ref, rev_ref, out_ref, 16 - k, 4 * chunk + 2 * i + 1, True)
+        slot = first + 2 * i
+        k = slot // 2
+        pack_rows(h_ref, swap_ref, rev_ref, out_ref, k, slot, False)
+        pack_rows(h_ref, swap_ref, rev_ref, out_ref, 16 - k, slot + 1, True)
         return 0
 
-    lax.fori_loop(0, 2, step, 0)
+    lax.fori_loop(0, count // 2, step, 0)
 
 
 def conv_block(big_ref, h_ref, tabs, g_ref, a_ref, k, slot, mirror):
@@ -320,7 +313,7 @@
             loads.append((h_hbm.at[ri, :, pl.ds(128 * half, 128)], big.at[pl.ds((2 * ri + half) * 4096, 4096), :]))
     loads += [(tw_hbm, tw_v), (hi_hbm, hi_v), (lo_hbm, lo_v), (cross_hbm, cross_v)]
     loads = [pltpu.make_async_copy(a, b, load_sems.at[i]) for i, (a, b) in enumerate(loads)]
-    for c in loads:
+    for c in loads[:4]:
         c.start()
     barrier = pltpu.get_barrier_semaphore()
     for peer in peers:
@@ -345,30 +338,37 @@
             c.wait_recv()
         pair[1].wait()
 
-    loads[0].wait()
-    loads[1].wait()
-    loads[2].wait()
-    pack_dy(grad_v, gate_v, swap_v, tok_send.at[0])
-    pl.semaphore_wait(barrier, 7)
-    dy_move = exchange(0, lambda d: tok_send.at[0, d], tok_recv.at[0, me])
+    halves = [pl.ds(256 * part, 256) for part in range(2)]
+    for c in loads[:3]:
+        c.wait()
+    dy_moves, val_moves, h_moves = [], [], []
+    for part in range(2):
+        pack_dy(grad_v, gate_v, swap_v, tok_send.at[0], part)
+        if part == 0:
+            pl.semaphore_wait(barrier, 7)
+        at = halves[part]
+        dy_moves.append(exchange(part, lambda d: tok_send.at[0, d, at], tok_recv.at[0, me, at]))
+    for c in loads[4:]:
+        c.start()
     loads[3].wait()
-    pack_values(val_v, swap_v, tok_send.at[1])
-    val_move = exchange(1, lambda d: tok_send.at[1, d], tok_recv.at[1, me])
+    for part in range(2):
+        pack_values(val_v, swap_v, tok_send.at[1], part)
+        at = halves[part]
+        val_moves.append(exchange(2 + part, lambda d: tok_send.at[1, d, at], tok_recv.at[1, me, at]))
     for c in loads[4:8]:
         c.wait()
-    h_moves = []
-    for chunk in range(4):
+    for chunk, (first, count) in enumerate(CHUNKS):
         pack_spectrum(big, swap_v, rev_ref, h_send, chunk)
-        part = pl.ds(4 * chunk, 4)
-        h_moves.append(exchange(2 + chunk, lambda d: h_send.at[d, part], h_recv.at[me, part]))
+        at = pl.ds(first, count)
+        h_moves.append(exchange(4 + chunk, lambda d: h_send.at[d, at], h_recv.at[me, at]))
     for c in loads[8:]:
         c.wait()
 
     tabs = (hi_v, lo_v, tw_v, lane_ref, cross_v)
-    arrived(dy_move)
-    forward_q(tok_recv.at[0], dy_a, lane_ref)
-    arrived(val_move)
-    forward_q(tok_recv.at[1], val_a, lane_ref)
+    for n, (moves, a_ref) in enumerate(((dy_moves, dy_a), (val_moves, val_a))):
+        for part in range(2):
+            arrived(moves[part])
+            forward_q(tok_recv.at[n], a_ref, lane_ref, part)
 
     def block(k, _):
         dy_s = forward_k(dy_a, k, tabs, dy_g)
@@ -389,26 +389,33 @@
             res_send[n, q, rows, :] = value.astype(BF16)
         return emit
 
-    inverse_q(big, emit_to(0), 0.5, 2.0 / N)
-    corr_move = exchange(6, lambda d: res_send.at[0, d], corr_out.at[me])
-
-    for chunk in range(4):
+    for part in range(2):
+        inverse_q(big, emit_to(0), 0.5, 2.0 / N, part)
+
+    conv_moves = []
+    for chunk, (first, count) in enumerate(CHUNKS):
         arrived(h_moves[chunk])
-        if chunk == 0:
+        if chunk == CORR_AFTER:
+            corr_move = exchange(9, lambda d: res_send.at[0, d], corr_out.at[me])
+        if first == 0:
             conv_block(big, h_recv, tabs, inv_g, inv_a, 0, 0, None)
             conv_block(big, h_recv, tabs, inv_g, inv_a, 8, 1, None)
-            conv_block(big, h_recv, tabs, inv_g, inv_a, 1, 2, 3)
-        else:
-            def step(i, _, chunk=chunk):
-                slot = 4 * chunk + 2 * i
-                conv_block(big, h_recv, tabs, inv_g, inv_a, 2 * chunk + i, slot, slot + 1)
-                return 0
-            lax.fori_loop(0, 2, step, 0)
-    inverse_q(big, emit_to(1), 1.0, 1.0 / N)
-    conv_move = exchange(7, lambda d: res_send.at[1, d], conv_out.at[me])
-    arrived(corr_move)
-    arrived(conv_move)
-    for pair in (dy_move, val_move, *h_moves, corr_move, conv_move):
+            first, count = 2, count - 2
+
+        def step(i, _, first=first):
+            slot = first + 2 * i
+            conv_block(big, h_recv, tabs, inv_g, inv_a, slot // 2, slot, slot + 1)
+            return 0
+
+        lax.fori_loop(0, count // 2, step, 0)
+    for part in range(2):
+        inverse_q(big, emit_to(1), 1.0, 1.0 / N, part)
+        at = halves[part]
+        conv_moves.append(exchange(10 + part, lambda d: res_send.at[1, d, at], conv_out.at[me, at]))
+    moves = (*dy_moves, *val_moves, *h_moves, corr_move, *conv_moves)
+    for pair in (corr_move, *conv_moves):
+        arrived(pair)
+    for pair in moves:
         for c in pair[0]:
             c.wait_send()
 
@@ -418,7 +425,7 @@
     hi, lo, tw, lane, cross, swap, rev = (jnp.asarray(a) for a in tables())
     anywhere = pl.BlockSpec(memory_space=pl.ANY)
     vmem = pl.BlockSpec(memory_space=pltpu.VMEM)
-    result = S_((8, 512, 128), BF16)
+    result = pltpu.VMEM((8, 512, 128), BF16)
     tokens = pltpu.VMEM((2048, 256), BF16)
     corr, conv = pl.pallas_call(
         main_kernel,
@@ -447,9 +454,9 @@
             pltpu.VMEM((2, 512, 256), BF16),
             pltpu.VMEM((2, 8, 512, 128), BF16),
             pltpu.SemaphoreType.DMA((12,)),
-            pltpu.SemaphoreType.DMA((8,)),
-            pltpu.SemaphoreType.DMA((8, 7)),
-            pltpu.SemaphoreType.DMA((8, 7)),
+            pltpu.SemaphoreType.DMA((12,)),
+            pltpu.SemaphoreType.DMA((12, 7)),
+            pltpu.SemaphoreType.DMA((12, 7)),
         ],
         compiler_params=pltpu.CompilerParams(collective_id=0, has_side_effects=True, vmem_limit_bytes=58 << 20),
     )(grad_out, gate, values, filter_spectrum, hi, lo, tw, cross, swap, lane, rev)

time: 112 us -> 108 us (0.964)
  local copies, waits for them, and re-layouts: 2.47 us -> 0.02 us
    unnamed x14 -> x10, local copies, waits for them, and re-layouts: 2.47 us -> 0.02 us
    pallas_call x1, Pallas kernels: 103 us -> 102 us  [on_device(): pl.pallas_call(main_kernel, out_shape=(result, result), in_specs=[anywher...]
where the time goes in v3:
time: 108 us; the launch traced here: 106 us
  Pallas kernels  106 us (98%)
    pallas_call x1, Pallas kernels, on_device(): pl.pallas_call(main_kernel, out_shape=(result, result), in_specs=[anywher...  102 us
    pallas_call x1, Pallas kernels, on_device(): pl.pallas_call(unpack_kernel, grid=(512 // rows,), out_shape=(S_((4, 512,...  3.85 us

profile of v3, /device:TPU:22, one launch (start us, length us, event | category | flops | bytes accessed | tf_op | source)
XLA Modules:
  0.0 106.5 jit_solution(11390896977361519108)
XLA Ops:
  0.6 0.0 copy-start
  0.6 0.0 copy-start.1
  0.7 0.0 copy-start.2
  0.7 0.0 copy-start.3
  0.7 0.0 copy-start.4
  0.7 101.9 %shard_map.148 = (bf16[8,512,128]{2,1,0:T(8,128)(2,1)S(1)}, bf16[8,512,128]{2,1,0:T(8,128)(2,1)S(1)}) custom-call(bf16[2048,256]{1,0:T(8,128)(2,1)} %grad_hbm.1, bf16[2048,256]{1,0:T(8,128)(2,1)} %gate_hbm.1, bf16[2048,256]{1,0:T(8,128)(2,1)} %val_hbm.1, f32[2,4096,256]{2,1,0:T(8,128)} %h_hbm.1, bf16[512,512]{1,0:T(8,128)(2,1)} %constant.14.clone.hi_hbm, ...), custom_call_target="tpu_custom_call" | custom-call | tf_op jit(solution)/shard_map/pallas_call | solution.py:430
  102.6 0.0 copy-done
  102.6 0.0 copy-done.1
  102.6 0.0 copy-done.2
  102.6 0.0 copy-done.3
  102.6 0.0 copy-done.4
  102.6 3.9 %shard_map.149 = (f32[4,512,256]{2,1,0:T(8,128)}, bf16[4,512,256]{2,1,0:T(8,128)(2,1)}, f32[4,512,256]{2,1,0:T(8,128)}) custom-call(bf16[8,512,128]{2,1,0:T(8,128)(2,1)S(1)} %get-tuple-element.8.conv_ref, bf16[8,512,128]{2,1,0:T(8,128)(2,1)S(1)} %get-tuple-element.9.corr_ref, bf16[4,512,256]{2,1,0:T(8,128)(2,1)S(1)} %bitcast.7, ...), custom_call_target="tpu_custom_call" | custom-call | tf_op jit(solution)/shard_map/pallas_call | solution.py:469
Async XLA Ops:
  0.6 101.9 %copy-start = (bf16[2048,256]{1,0:T(8,128)(2,1)S(1)}, bf16[2048,256]{1,0:T(8,128)(2,1)}, u32[]{:S(2)}) copy-start(bf16[2048,256]{1,0:T(8,128)(2,1)} %grad_hbm.1) | copy-start | bytes 3145732
  0.6 101.9 %copy-start.1 = (bf16[2048,256]{1,0:T(8,128)(2,1)S(1)}, bf16[2048,256]{1,0:T(8,128)(2,1)}, u32[]{:S(2)}) copy-start(bf16[2048,256]{1,0:T(8,128)(2,1)} %gate_hbm.1) | copy-start | bytes 3145732
  0.7 101.9 %copy-start.2 = (bf16[512,512]{1,0:T(8,128)(2,1)S(1)}, bf16[512,512]{1,0:T(8,128)(2,1)}, u32[]{:S(2)}) copy-start(bf16[512,512]{1,0:T(8,128)(2,1)} %constant.19.clone.swap_hbm.swap_ref) | copy-start | bytes 1572868
  0.7 101.9 %copy-start.3 = (bf16[2048,256]{1,0:T(8,128)(2,1)S(1)}, bf16[2048,256]{1,0:T(8,128)(2,1)}, u32[]{:S(2)}) copy-start(bf16[2048,256]{1,0:T(8,128)(2,1)} %param.16) | copy-start | bytes 3145732
  0.7 101.9 %copy-start.4 = (f32[256]{0:T(256)S(1)}, f32[256]{0:T(256)}, u32[]{:S(2)}) copy-start(f32[256]{0:T(256)} %param.18) | copy-start | bytes 3076

commit v4 on v3

--- a/solution.py
+++ b/solution.py
@@ -298,26 +298,26 @@
 
 
 def main_kernel(
-    grad_hbm, gate_hbm, val_hbm, h_hbm, hi_hbm, lo_hbm, tw_hbm, cross_hbm, swap_hbm, lane_ref, rev_ref,
+    grad_hbm, gate_hbm, val_hbm, h_hbm, hi_hbm, lo_hbm, tw_hbm, cross_hbm, swap_hbm, lane_hbm, rev_hbm,
     corr_out, conv_out,
-    grad_v, gate_v, val_v, hi_v, lo_v, tw_v, cross_v, swap_v, tok_send, tok_recv, h_send, h_recv,
+    grad_v, gate_v, val_v, hi_v, lo_v, tw_v, cross_v, swap_v, lane_v, rev_v, tok_send, tok_recv, h_send, h_recv,
     big, dy_a, val_a, inv_a, dy_g, val_g, inv_g, res_send, load_sems, own_sems, send_sems, recv_sems,
 ):
     me = lax.axis_index("ctx")
     x, z = me // 2, me % 2
     peers = [((x + dx) % 4) * 2 + (z + dz) % 2 for dx, dz in OFFSETS]
 
+    barrier = pltpu.get_barrier_semaphore()
+    for peer in peers:
+        pl.semaphore_signal(barrier, inc=1, device_id={"ctx": peer}, device_id_type=MESH)
     loads = [(grad_hbm, grad_v), (gate_hbm, gate_v), (swap_hbm, swap_v), (val_hbm, val_v)]
     for ri in range(2):
         for half in range(2):
             loads.append((h_hbm.at[ri, :, pl.ds(128 * half, 128)], big.at[pl.ds((2 * ri + half) * 4096, 4096), :]))
-    loads += [(tw_hbm, tw_v), (hi_hbm, hi_v), (lo_hbm, lo_v), (cross_hbm, cross_v)]
+    loads += [(rev_hbm, rev_v), (lane_hbm, lane_v), (tw_hbm, tw_v), (hi_hbm, hi_v), (lo_hbm, lo_v), (cross_hbm, cross_v)]
     loads = [pltpu.make_async_copy(a, b, load_sems.at[i]) for i, (a, b) in enumerate(loads)]
     for c in loads[:4]:
         c.start()
-    barrier = pltpu.get_barrier_semaphore()
-    for peer in peers:
-        pl.semaphore_signal(barrier, inc=1, device_id={"ctx": peer}, device_id_type=MESH)
 
     def exchange(group, source, target):
         copies = []
@@ -342,33 +342,31 @@
     for c in loads[:3]:
         c.wait()
     dy_moves, val_moves, h_moves = [], [], []
-    for part in range(2):
+    for part, at in enumerate(halves):
         pack_dy(grad_v, gate_v, swap_v, tok_send.at[0], part)
         if part == 0:
             pl.semaphore_wait(barrier, 7)
-        at = halves[part]
         dy_moves.append(exchange(part, lambda d: tok_send.at[0, d, at], tok_recv.at[0, me, at]))
     for c in loads[4:]:
         c.start()
     loads[3].wait()
-    for part in range(2):
+    for part, at in enumerate(halves):
         pack_values(val_v, swap_v, tok_send.at[1], part)
-        at = halves[part]
         val_moves.append(exchange(2 + part, lambda d: tok_send.at[1, d, at], tok_recv.at[1, me, at]))
-    for c in loads[4:8]:
+    for c in loads[4:9]:
         c.wait()
     for chunk, (first, count) in enumerate(CHUNKS):
-        pack_spectrum(big, swap_v, rev_ref, h_send, chunk)
+        pack_spectrum(big, swap_v, rev_v, h_send, chunk)
         at = pl.ds(first, count)
         h_moves.append(exchange(4 + chunk, lambda d: h_send.at[d, at], h_recv.at[me, at]))
-    for c in loads[8:]:
+    for c in loads[9:]:
         c.wait()
 
-    tabs = (hi_v, lo_v, tw_v, lane_ref, cross_v)
+    tabs = (hi_v, lo_v, tw_v, lane_v, cross_v)
     for n, (moves, a_ref) in enumerate(((dy_moves, dy_a), (val_moves, val_a))):
         for part in range(2):
             arrived(moves[part])
-            forward_q(tok_recv.at[n], a_ref, lane_ref, part)
+            forward_q(tok_recv.at[n], a_ref, lane_v, part)
 
     def block(k, _):
         dy_s = forward_k(dy_a, k, tabs, dy_g)
@@ -424,13 +422,12 @@
     S_ = jax.ShapeDtypeStruct
     hi, lo, tw, lane, cross, swap, rev = (jnp.asarray(a) for a in tables())
     anywhere = pl.BlockSpec(memory_space=pl.ANY)
-    vmem = pl.BlockSpec(memory_space=pltpu.VMEM)
     result = pltpu.VMEM((8, 512, 128), BF16)
     tokens = pltpu.VMEM((2048, 256), BF16)
     corr, conv = pl.pallas_call(
         main_kernel,
         out_shape=(result, result),
-        in_specs=[anywhere] * 9 + [vmem] * 2,
+        in_specs=[anywhere] * 11,
         out_specs=(anywhere, anywhere),
         scratch_shapes=[
             tokens,
@@ -441,6 +438,8 @@
             pltpu.VMEM((9, 512, 256), F32),
             pltpu.VMEM((2, 512, 256), BF16),
             pltpu.VMEM((512, 512), BF16),
+            pltpu.VMEM((9, 8, 128), F32),
+            pltpu.VMEM((64, 64), BF16),
             pltpu.VMEM((2, 8, 512, 128), BF16),
             pltpu.VMEM((2, 8, 512, 128), BF16),
             pltpu.VMEM((8, 16, 2, 64, 128), BF16),
@@ -453,7 +452,7 @@
             pltpu.VMEM((2, 512, 256), BF16),
             pltpu.VMEM((2, 512, 256), BF16),
             pltpu.VMEM((2, 8, 512, 128), BF16),
-            pltpu.SemaphoreType.DMA((12,)),
+            pltpu.SemaphoreType.DMA((14,)),
             pltpu.SemaphoreType.DMA((12,)),
             pltpu.SemaphoreType.DMA((12, 7)),
             pltpu.SemaphoreType.DMA((12, 7)),
@@ -461,7 +460,7 @@
         compiler_params=pltpu.CompilerParams(collective_id=0, has_side_effects=True, vmem_limit_bytes=58 << 20),
     )(grad_out, gate, values, filter_spectrum, hi, lo, tw, cross, swap, lane, rev)
 
-    rows = 128
+    rows = 256
     packed = pl.BlockSpec((8, rows, 128), lambda i: (0, i, 0))
     plain = pl.BlockSpec((4, rows, 256), lambda i: (0, i, 0))
     whole = lambda shape: pl.BlockSpec(shape, lambda i: (0, 0))

time: 108 us -> 107 us (level)
  no operation moved by 1% of the time
where the time goes in v4:
time: 107 us; the launch traced here: 105 us
  Pallas kernels  105 us (98%)
    pallas_call x1, Pallas kernels, on_device(): pl.pallas_call(main_kernel, out_shape=(result, result), in_specs=[anywher...  101 us
    pallas_call x1, Pallas kernels, on_device(): pl.pallas_call(unpack_kernel, grid=(512 // rows,), out_shape=(S_((4, 512,...  3.52 us

profile of v4, /device:TPU:22, one launch (start us, length us, event | category | flops | bytes accessed | tf_op | source)
XLA Modules:
  0.0 105.4 jit_solution(11531690850226748641)
XLA Ops:
  0.6 0.0 copy-start
  0.6 0.0 copy-start.1
  0.7 0.0 copy-start.2
  0.7 0.0 copy-start.3
  0.7 0.0 copy-start.4
  0.7 101.2 %shard_map.148 = (bf16[8,512,128]{2,1,0:T(8,128)(2,1)S(1)}, bf16[8,512,128]{2,1,0:T(8,128)(2,1)S(1)}) custom-call(bf16[2048,256]{1,0:T(8,128)(2,1)} %grad_hbm.1, bf16[2048,256]{1,0:T(8,128)(2,1)} %gate_hbm.1, bf16[2048,256]{1,0:T(8,128)(2,1)} %val_hbm.1, f32[2,4096,256]{2,1,0:T(8,128)} %h_hbm.1, bf16[512,512]{1,0:T(8,128)(2,1)} %constant.14.clone.hi_hbm, ...), custom_call_target="tpu_custom_call" | custom-call | tf_op jit(solution)/shard_map/pallas_call | solution.py:427
  101.9 0.0 copy-done
  101.9 0.0 copy-done.1
  101.9 0.0 copy-done.2
  101.9 0.0 copy-done.3
  101.9 0.0 copy-done.4
  101.9 3.5 %shard_map.149 = (f32[4,512,256]{2,1,0:T(8,128)}, bf16[4,512,256]{2,1,0:T(8,128)(2,1)}, f32[4,512,256]{2,1,0:T(8,128)}) custom-call(bf16[8,512,128]{2,1,0:T(8,128)(2,1)S(1)} %get-tuple-element.8.conv_ref, bf16[8,512,128]{2,1,0:T(8,128)(2,1)S(1)} %get-tuple-element.9.corr_ref, bf16[4,512,256]{2,1,0:T(8,128)(2,1)S(1)} %bitcast.7, ...), custom_call_target="tpu_custom_call" | custom-call | tf_op jit(solution)/shard_map/pallas_call | solution.py:468
Async XLA Ops:
  0.6 101.2 %copy-start = (bf16[2048,256]{1,0:T(8,128)(2,1)S(1)}, bf16[2048,256]{1,0:T(8,128)(2,1)}, u32[]{:S(2)}) copy-start(bf16[2048,256]{1,0:T(8,128)(2,1)} %grad_hbm.1) | copy-start | bytes 3145732
  0.6 101.2 %copy-start.1 = (bf16[2048,256]{1,0:T(8,128)(2,1)S(1)}, bf16[2048,256]{1,0:T(8,128)(2,1)}, u32[]{:S(2)}) copy-start(bf16[2048,256]{1,0:T(8,128)(2,1)} %gate_hbm.1) | copy-start | bytes 3145732
  0.7 101.2 %copy-start.2 = (bf16[512,512]{1,0:T(8,128)(2,1)S(1)}, bf16[512,512]{1,0:T(8,128)(2,1)}, u32[]{:S(2)}) copy-start(bf16[512,512]{1,0:T(8,128)(2,1)} %constant.19.clone.swap_hbm.swap_ref) | copy-start | bytes 1572868
  0.7 101.2 %copy-start.3 = (bf16[2048,256]{1,0:T(8,128)(2,1)S(1)}, bf16[2048,256]{1,0:T(8,128)(2,1)}, u32[]{:S(2)}) copy-start(bf16[2048,256]{1,0:T(8,128)(2,1)} %param.16) | copy-start | bytes 3145732
  0.7 101.2 %copy-start.4 = (f32[256]{0:T(256)S(1)}, f32[256]{0:T(256)}, u32[]{:S(2)}) copy-start(f32[256]{0:T(256)} %param.18) | copy-start | bytes 3076
